TPU v7x, 32 devices: a whole 2x2x4 slice. The times are simulated.
32 devices in a mesh: seq: 8 (over z, y), dp: 4 (over x, core).
Axes of the slice: x: 2, y: 2, z: 4, core: 2. Of those that a mesh axis runs over, the one named last changes fastest.
Arguments:
- layer_inputs: bfloat16 [4, 2048, 4096], P('dp', 'seq')
- doc_start: int32 [4, 2048], P('dp', 'seq'), may hold values from 0 to 2047, as said below
- w_qkv: bfloat16 [4096, 512], P(('seq', 'dp'))
- d_context: bfloat16 [4, 2048, 256], P('dp', 'seq'), may hold values from -6 to 6
Outputs:
- d_x: bfloat16 [4, 2048, 4096], P('dp', 'seq')
- g_qkv: float32 [4096, 512], P(('seq', 'dp'))
Inputs may be any that keep to these rules, and one draw needn't show every extreme that they name: doc_start[g, i] is at most i, never falls along positions, doc_start[g, 0] = 0, and doc_start[g, doc_start[g, i]] = doc_start[g, i].
All inputs are finite; a program needn't handle non-finite values.
Results may differ from a plain program's by a relative error of at most 0.017.
Values may be sent and summed in bfloat16 or wider, within the bound.
A program may use at most 64 MiB of HBM per device.

v0:
```python
import jax
import jax.numpy as jnp
from jax import lax
from jax.sharding import PartitionSpec as P

WIN = 256


def from_partner(block, axis, stride):
    count = lax.axis_size(axis)
    route = []
    for low in range(count):
        high = low | 1 << stride
        if high != low and high < count:
            route += [(low, high), (high, low)]
    return lax.ppermute(block, axis, route)


def from_behind(block, axis, distance):
    devices = range(lax.axis_size(axis))
    route = [(i - distance, i) for i in devices if i - distance in devices]
    return lax.ppermute(block, axis, route)


def masked_scores(queries, key_rows, doc_first, query_pos, key_pos):
    inv_root = queries.shape[2] ** (-0.5)
    scores = (
        jnp.einsum("rhd,kd->hrk", queries, key_rows, preferred_element_type=jnp.float32) * inv_root
    )
    visible = (
        (key_pos[None, :] <= query_pos[:, None])
        & (key_pos[None, :] > query_pos[:, None] - WIN)
        & (key_pos[None, :] >= doc_first[:, None])
    )
    return jnp.where(visible[None, :, :], scores, -jnp.inf)


def backward_terms(queries, key_rows, value_rows, out_grad, attn_probs, prob_low, row_dot):
    inv_root = queries.shape[2] ** (-0.5)
    prob_grad = jnp.einsum("rhd,kd->hrk", out_grad, value_rows, preferred_element_type=jnp.float32)
    score_grad = (attn_probs * (prob_grad - row_dot[:, :, None])).astype(jnp.bfloat16)
    grad_query = (
        jnp.einsum("hrk,kd->rhd", score_grad, key_rows, preferred_element_type=jnp.float32)
        * inv_root
    )
    grad_keys = (
        jnp.einsum("hrk,rhd->kd", score_grad, queries, preferred_element_type=jnp.float32)
        * inv_root
    )
    grad_values = jnp.einsum("hrk,rhd->kd", prob_low, out_grad, preferred_element_type=jnp.float32)
    return (grad_query, grad_keys, grad_values)


def local_pass(queries, key_rows, value_rows, out_grad, doc_first, query_pos, key_pos):
    scores = masked_scores(queries, key_rows, doc_first, query_pos, key_pos)
    row_max = jnp.max(scores, axis=2)
    log_total = row_max + jnp.log(jnp.sum(jnp.exp(scores - row_max[:, :, None]), axis=2))
    attn_probs = jnp.exp(scores - log_total[:, :, None])
    prob_low = attn_probs.astype(jnp.bfloat16)
    context = jnp.einsum("hrk,kd->rhd", prob_low, value_rows, preferred_element_type=jnp.float32)
    row_dot = jnp.sum(out_grad.astype(jnp.float32) * context, axis=2).T
    grad_query, grad_keys, grad_values = backward_terms(
        queries, key_rows, value_rows, out_grad, attn_probs, prob_low, row_dot
    )
    return (grad_query, grad_keys, grad_values, log_total, row_dot)


def halve_over_seq(buffer, bit_index):
    half_rows = buffer.shape[0] // 2
    my_bit = lax.axis_index("seq") >> bit_index & 1
    kept_half = lax.dynamic_slice_in_dim(buffer, my_bit * half_rows, half_rows, 0)
    sent_half = lax.dynamic_slice_in_dim(buffer, (1 - my_bit) * half_rows, half_rows, 0)
    return kept_half + from_partner(sent_half.astype(jnp.bfloat16), "seq", bit_index).astype(
        sent_half.dtype
    )


def halve_over_dp(buffer, bit_index):
    half_rows = buffer.shape[0] // 2
    my_bit = lax.axis_index("dp") >> bit_index & 1
    kept_half = lax.dynamic_slice_in_dim(buffer, my_bit * half_rows, half_rows, 0)
    sent_half = lax.dynamic_slice_in_dim(buffer, (1 - my_bit) * half_rows, half_rows, 0)
    return kept_half + from_partner(sent_half.astype(jnp.bfloat16), "dp", bit_index).astype(
        sent_half.dtype
    )


def body(layer_inputs, doc_start, w_qkv, d_context):
    x_local = layer_inputs[0]
    tok_rows = x_local.shape[0]
    q_width = d_context.shape[2]
    head_dim = (w_qkv.shape[1] - q_width) // 2
    heads = q_width // head_dim
    out_grad = d_context[0].reshape(tok_rows, heads, head_dim)
    doc_first = doc_start[0]
    positions = lax.axis_index("seq") * tok_rows + jnp.arange(tok_rows, dtype=jnp.int32)
    full_weights = lax.all_gather(w_qkv, ("seq", "dp"), axis=0, tiled=True)
    projected = jnp.dot(x_local, full_weights, preferred_element_type=jnp.float32)
    projected = projected.astype(jnp.bfloat16)
    queries = projected[:, :q_width].reshape(tok_rows, heads, head_dim)
    key_value = projected[:, q_width:]
    prior = from_behind(key_value, "seq", 1)
    key_rows = jnp.concatenate([prior[:, :head_dim], key_value[:, :head_dim]], axis=0)
    value_rows = jnp.concatenate([prior[:, head_dim:], key_value[:, head_dim:]], axis=0)
    key_pos = jnp.concatenate([positions - tok_rows, positions])
    grad_query, grad_keys, grad_values, log_total, row_dot = local_pass(
        queries, key_rows, value_rows, out_grad, doc_first, positions, key_pos
    )
    returned = from_behind(
        jnp.concatenate([grad_keys[:tok_rows], grad_values[:tok_rows]], axis=1).astype(
            jnp.bfloat16
        ),
        "seq",
        -1,
    ).astype(jnp.float32)
    far_keys = returned[:, :head_dim]
    far_values = returned[:, head_dim:]
    key_grad = (grad_keys[tok_rows:] + far_keys).astype(jnp.bfloat16)
    value_grad = (grad_values[tok_rows:] + far_values).astype(jnp.bfloat16)
    grad_proj = jnp.concatenate(
        [grad_query.astype(jnp.bfloat16).reshape(tok_rows, q_width), key_grad, value_grad], axis=1
    )
    input_grad = lax.dot_general(
        grad_proj, full_weights, (((1,), (1,)), ((), ())), preferred_element_type=jnp.float32
    )
    input_grad = input_grad.astype(jnp.bfloat16).reshape(1, tok_rows, x_local.shape[1])
    partial_grad = lax.dot_general(
        x_local, grad_proj, (((0,), (0,)), ((), ())), preferred_element_type=jnp.float32
    )
    seq_count = lax.axis_size("seq")
    dp_count = lax.axis_size("dp")
    seq_levels = seq_count.bit_length() - 1
    dp_levels = dp_count.bit_length() - 1
    buffer = partial_grad
    for bit_index in range(seq_levels - 1, -1, -1):
        buffer = halve_over_seq(buffer, bit_index)
    for bit_index in range(dp_levels - 1, -1, -1):
        buffer = halve_over_dp(buffer, bit_index)
    return (input_grad, buffer)


def solution(mesh):
    return jax.shard_map(
        body,
        mesh=mesh,
        in_specs=(
            P("dp", "seq", None),
            P("dp", "seq"),
            P(("seq", "dp"), None),
            P("dp", "seq", None),
        ),
        out_specs=(P("dp", "seq", None), P(("seq", "dp"), None)),
        check_vma=False,
    )
```

profile of v0, /device:TPU:0, one launch (start us, length us, event | category | flops | bytes accessed | tf_op | source)
XLA Modules:
  0.0 264.4 jit_solution(14438567470808105061)
XLA Ops:
  7.2 0.0 copy-start
  7.2 0.0 all-gather.2.cloned.1.call-start
  7.2 0.7 all-gather.2.cloned.1.call-update
  7.9 1.0 copy.7
  9.0 0.9 compare_and_fusion
  9.9 65.8 %all-gather.2.cloned.1.call-done = bf16[4096,512]{1,0:T(8,128)(2,1)} async-done(((bf16[128,512]{1,0:T(8,128)(2,1)}), bf16[4096,512]{1,0:T(8,128)(2,1)}) %all-gather.2.cloned.1.call-update) | async-done | bytes 4194320 | tf_op jit(solution)/shard_map/all_gather | solution.py:97
  75.6 0.0 copy-done
  75.6 3.4 %fusion.11 = bf16[256,512]{1,0:T(8,128)(2,1)S(1)} fusion(bf16[4096,512]{1,0:T(8,128)(2,1)} %all-gather.2.cloned.1.call-done, bf16[1,256,4096]{2,1,0:T(8,128)(2,1)S(1)} %copy-done), kind=kOutput, calls=%fused_computation.18 | convolution fusion | flops 1073872896 | bytes 6553600 | tf_op jit(solution)/shard_map/dot_general | solution.py:98
  79.1 0.1 copy.26
  79.2 3.4 %collective-permute-start = (bf16[256,256]{1,0:T(8,128)(2,1)S(1)}, bf16[256,256]{1,0:T(8,128)(2,1)S(1)}, u32[]{:S(2)}, u32[]{:S(2)}) collective-permute-start(bf16[256,256]{1,0:T(8,128)(2,1)S(1)} %get-tuple-element.8), channel_id=1, source_target_pairs={{0,4},{4,8},{8,12},{12,16},{16,20},{20,24},{24,28},{1,5},{5,9},{9,... | collective-permute-start | bytes 393224 | tf_op jit(solution)/shard_map/ppermute | solution.py:22
  82.6 3.1 %collective-permute-done = bf16[256,256]{1,0:T(8,128)(2,1)S(1)} collective-permute-done((bf16[256,256]{1,0:T(8,128)(2,1)S(1)}, bf16[256,256]{1,0:T(8,128)(2,1)S(1)}, u32[]{:S(2)}, u32[]{:S(2)}) %collective-permute-start) | collective-permute-done | bytes 131104 | tf_op jit(solution)/shard_map/ppermute | solution.py:22
  85.8 0.3 fusion.32
  86.1 0.2 exponential_reduce_fusion
  86.3 0.3 convolution_bitcast_fusion.1
  86.6 0.3 fusion.17
  86.9 0.3 fusion.10
  87.2 0.3 fusion.14
  87.6 1.3 collective-permute-start.1
  88.9 0.3 fusion.16
  89.2 5.9 %collective-permute-done.1 = bf16[256,256]{0,1:T(8,128)(2,1)S(1)} collective-permute-done((bf16[256,256]{0,1:T(8,128)(2,1)S(1)}, bf16[256,256]{0,1:T(8,128)(2,1)S(1)}, u32[]{:S(2)}, u32[]{:S(2)}) %collective-permute-start.1) | collective-permute-done | bytes 131104 | tf_op jit(solution)/shard_map/ppermute | solution.py:22
  95.2 1.3 fusion.2
  96.4 0.0 copy-start.1
  96.4 3.2 %copy-done.1 = f32[512,4096]{1,0:T(8,128)} copy-done((f32[512,4096]{1,0:T(8,128)}, f32[512,4096]{1,0:T(8,128)S(1)}, u32[]{:S(2)}) %copy-start.1) | copy-done | bytes 8388632
  99.6 1.6 fusion.1
  101.3 2.9 %collective-permute-start.2 = (bf16[2048,512]{0,1:T(8,128)(2,1)}, bf16[2048,512]{0,1:T(8,128)(2,1)}, u32[]{:S(2)}, u32[]{:S(2)}) collective-permute-start(bf16[2048,512]{0,1:T(8,128)(2,1)} %fusion.1), channel_id=1, source_target_pairs={{0,16},{16,0},{4,20},{20,4},{8,24},{24,8},{12,28},{28,12},{1,17},{... | collective-permute-start | bytes 6291464 | tf_op jit(solution)/shard_map/ppermute | solution.py:16
  104.2 89.6 %collective-permute-done.2 = bf16[2048,512]{0,1:T(8,128)(2,1)} collective-permute-done((bf16[2048,512]{0,1:T(8,128)(2,1)}, bf16[2048,512]{0,1:T(8,128)(2,1)}, u32[]{:S(2)}, u32[]{:S(2)}) %collective-permute-start.2) | collective-permute-done | bytes 2097184 | tf_op jit(solution)/shard_map/ppermute | solution.py:16
  193.8 3.4 %bitcast_add_fusion = f32[2048,512]{0,1:T(8,128)S(1)} fusion(bf16[2048,512]{0,1:T(8,128)(2,1)} %collective-permute-done.2, f32[512,4096]{1,0:T(8,128)} %copy-done.1, s32[]{:T(128)S(6)} %select_n.35), kind=kLoop, calls=%fused_computation.2 | loop fusion | flops 2097152 | bytes 10485764 | tf_op jit(solution)/shard_map/add | solution.py:73
  197.2 0.0 copy-start.2
  197.2 1.9 copy-done.2
  199.2 0.2 dynamic-slice_convert_fusion.1
  199.3 0.1 collective-permute-start.3
  199.4 23.5 %collective-permute-done.3 = bf16[1024,512]{0,1:T(8,128)(2,1)} collective-permute-done((bf16[1024,512]{0,1:T(8,128)(2,1)S(1)}, bf16[1024,512]{0,1:T(8,128)(2,1)}, u32[]{:S(2)}, u32[]{:S(2)}) %collective-permute-start.3) | collective-permute-done | bytes 1048608 | tf_op jit(solution)/shard_map/ppermute | solution.py:16
  222.9 2.2 convert_add_fusion
  225.1 0.0 copy-start.3
  225.2 1.3 copy-done.3
  226.5 0.1 dynamic-slice_convert_fusion.2
  226.5 3.0 %collective-permute-start.4 = (bf16[512,512]{0,1:T(8,128)(2,1)S(1)}, bf16[512,512]{0,1:T(8,128)(2,1)}, u32[]{:S(2)}, u32[]{:S(2)}) collective-permute-start(bf16[512,512]{0,1:T(8,128)(2,1)S(1)} %dynamic-slice_convert_fusion.2), channel_id=1, source_target_pairs={{0,4},{4,0},{8,12},{12,8},{16,20},{20,16},{24,28},{28,24},{1,5},{5... | collective-permute-start | bytes 1572872 | tf_op jit(solution)/shard_map/ppermute | solution.py:16
  229.6 10.4 %collective-permute-done.4 = bf16[512,512]{0,1:T(8,128)(2,1)} collective-permute-done((bf16[512,512]{0,1:T(8,128)(2,1)S(1)}, bf16[512,512]{0,1:T(8,128)(2,1)}, u32[]{:S(2)}, u32[]{:S(2)}) %collective-permute-start.4) | collective-permute-done | bytes 524320 | tf_op jit(solution)/shard_map/ppermute | solution.py:16
  239.9 1.5 convert_add_fusion.1
  241.5 0.7 dynamic-slice_convert_fusion.3
  242.2 3.2 %collective-permute-start.5 = (bf16[256,512]{0,1:T(8,128)(2,1)}, bf16[256,512]{0,1:T(8,128)(2,1)}, u32[]{:S(2)}, u32[]{:S(2)}) collective-permute-start(bf16[256,512]{0,1:T(8,128)(2,1)} %dynamic-slice_convert_fusion.3), channel_id=1, source_target_pairs={{0,2},{2,0},{1,3},{3,1},{4,6},{6,4},{5,7},{7,5},{8,10},{10,8},{9,1... | collective-permute-start | bytes 786440 | tf_op jit(solution)/shard_map/ppermute | solution.py:16
  245.4 5.3 %collective-permute-done.5 = bf16[256,512]{0,1:T(8,128)(2,1)} collective-permute-done((bf16[256,512]{0,1:T(8,128)(2,1)}, bf16[256,512]{0,1:T(8,128)(2,1)}, u32[]{:S(2)}, u32[]{:S(2)}) %collective-permute-start.5) | collective-permute-done | bytes 262176 | tf_op jit(solution)/shard_map/ppermute | solution.py:16
  250.7 1.0 convert_add_fusion.2
  251.8 0.1 collective-permute-start.6
  251.8 4.8 %fusion = bf16[1,256,4096]{2,1,0:T(8,128)(2,1)} fusion(bf16[4096,512]{1,0:T(8,128)(2,1)} %all-gather.2.cloned.1.call-done, bf16[256,128]{0,1:T(8,128)(2,1)S(1)} %get-tuple-element.5, bf16[256,128]{0,1:T(8,128)(2,1)S(1)} %get-tuple-element.4, bf16[256,256]{0,1:T(8,128)(2,1)S(1)} %bitcast.68), kind=kOutput, calls=%fused_computation.1 | convolution fusion | flops 1075576832 | bytes 6553600 | tf_op jit(solution)/shard_map/dot_general | solution.py:123
  256.7 0.0 collective-permute-done.6
  256.7 0.8 copy.16
  (13 shorter events, 0.2 us)
Async XLA Ops:
  7.2 68.5 %copy-start = (bf16[1,256,4096]{2,1,0:T(8,128)(2,1)S(1)}, bf16[1,256,4096]{2,1,0:T(8,128)(2,1)}, u32[]{:S(2)}) copy-start(bf16[1,256,4096]{2,1,0:T(8,128)(2,1)} %param.4) | copy-start | bytes 6291460
  7.2 68.5 %all-gather.2.cloned.1.call-start = ((), (), s32[]{:S(2)}) async-start(), calls=%async_computation | async-start | bytes 4325376 | tf_op jit(solution)/shard_map/all_gather | solution.py:97
  79.2 6.6 %collective-permute-start = (bf16[256,256]{1,0:T(8,128)(2,1)S(1)}, bf16[256,256]{1,0:T(8,128)(2,1)S(1)}, u32[]{:S(2)}, u32[]{:S(2)}) collective-permute-start(bf16[256,256]{1,0:T(8,128)(2,1)S(1)} %get-tuple-element.8), channel_id=1, source_target_pairs={{0,4},{4,8},{8,12},{12,16},{16,20},{20,24},{24,28},{1,5},{5,9},{9,... | collective-permute-start | bytes 393224 | tf_op jit(solution)/shard_map/ppermute | solution.py:22
  87.6 7.5 %collective-permute-start.1 = (bf16[256,256]{0,1:T(8,128)(2,1)S(1)}, bf16[256,256]{0,1:T(8,128)(2,1)S(1)}, u32[]{:S(2)}, u32[]{:S(2)}) collective-permute-start(bf16[256,256]{0,1:T(8,128)(2,1)S(1)} %pad_maximum_fusion.1), channel_id=1, source_target_pairs={{4,0},{8,4},{12,8},{16,12},{20,16},{24,20},{28,24},{5,1},{9,5},{13... | collective-permute-start | bytes 393224 | tf_op jit(solution)/shard_map/ppermute | solution.py:22
  96.4 3.2 %copy-start.1 = (f32[512,4096]{1,0:T(8,128)}, f32[512,4096]{1,0:T(8,128)S(1)}, u32[]{:S(2)}) copy-start(f32[512,4096]{1,0:T(8,128)S(1)} %fusion.2) | copy-start | bytes 25165828
  101.3 92.5 %collective-permute-start.2 = (bf16[2048,512]{0,1:T(8,128)(2,1)}, bf16[2048,512]{0,1:T(8,128)(2,1)}, u32[]{:S(2)}, u32[]{:S(2)}) collective-permute-start(bf16[2048,512]{0,1:T(8,128)(2,1)} %fusion.1), channel_id=1, source_target_pairs={{0,16},{16,0},{4,20},{20,4},{8,24},{24,8},{12,28},{28,12},{1,17},{... | collective-permute-start | bytes 6291464 | tf_op jit(solution)/shard_map/ppermute | solution.py:16
  197.2 2.0 copy-start.2
  199.3 23.6 %collective-permute-start.3 = (bf16[1024,512]{0,1:T(8,128)(2,1)S(1)}, bf16[1024,512]{0,1:T(8,128)(2,1)}, u32[]{:S(2)}, u32[]{:S(2)}) collective-permute-start(bf16[1024,512]{0,1:T(8,128)(2,1)S(1)} %dynamic-slice_convert_fusion.1), channel_id=1, source_target_pairs={{0,8},{8,0},{4,12},{12,4},{16,24},{24,16},{20,28},{28,20},{1,9},{9... | collective-permute-start | bytes 3145736 | tf_op jit(solution)/shard_map/ppermute | solution.py:16
  225.1 1.3 copy-start.3
  226.5 13.4 %collective-permute-start.4 = (bf16[512,512]{0,1:T(8,128)(2,1)S(1)}, bf16[512,512]{0,1:T(8,128)(2,1)}, u32[]{:S(2)}, u32[]{:S(2)}) collective-permute-start(bf16[512,512]{0,1:T(8,128)(2,1)S(1)} %dynamic-slice_convert_fusion.2), channel_id=1, source_target_pairs={{0,4},{4,0},{8,12},{12,8},{16,20},{20,16},{24,28},{28,24},{1,5},{5... | collective-permute-start | bytes 1572872 | tf_op jit(solution)/shard_map/ppermute | solution.py:16
  242.2 8.5 %collective-permute-start.5 = (bf16[256,512]{0,1:T(8,128)(2,1)}, bf16[256,512]{0,1:T(8,128)(2,1)}, u32[]{:S(2)}, u32[]{:S(2)}) collective-permute-start(bf16[256,512]{0,1:T(8,128)(2,1)} %dynamic-slice_convert_fusion.3), channel_id=1, source_target_pairs={{0,2},{2,0},{1,3},{3,1},{4,6},{6,4},{5,7},{7,5},{8,10},{10,8},{9,1... | collective-permute-start | bytes 786440 | tf_op jit(solution)/shard_map/ppermute | solution.py:16
  251.8 4.9 %collective-permute-start.6 = (bf16[128,512]{0,1:T(8,128)(2,1)S(1)}, bf16[128,512]{0,1:T(8,128)(2,1)S(1)}, u32[]{:S(2)}, u32[]{:S(2)}) collective-permute-start(bf16[128,512]{0,1:T(8,128)(2,1)S(1)} %dynamic-slice_convert_fusion.4), channel_id=1, source_target_pairs={{0,1},{1,0},{2,3},{3,2},{4,5},{5,4},{6,7},{7,6},{8,9},{9,8},{10,11... | collective-permute-start | bytes 393224 | tf_op jit(solution)/shard_map/ppermute | solution.py:16
Sparse Core Ops, SparseCore 0:
  10.9 64.7 all-gather.1
where the time goes:
time: 265 us; the launch traced here: 264 us
  waiting for transfers between devices  204 us (77%)
  between operations  14.3 us (5%)
  starting transfers between devices  14 us (5%)
  matrix products  11.3 us (4%)
  local copies, waits for them, and re-layouts  11.1 us (4%)
  other arithmetic  9.38 us (4%)
    ppermute x5, waiting for transfers between devices, from_partner(): return lax.ppermute(block, axis, route)  129 us
    all_gather x1, waiting for transfers between devices, body(): full_weights = lax.all_gather(w_qkv, ('seq', 'dp'), axis=0, tiled=True)  65.8 us
    ppermute x5, starting transfers between devices, from_partner(): return lax.ppermute(block, axis, route)  9.27 us
    ppermute x2, waiting for transfers between devices, from_behind(): return lax.ppermute(block, axis, route)  9.07 us
    unnamed x10, local copies, waits for them, and re-layouts  8.32 us
    add x3, other arithmetic, halve_over_seq(): kept_half + from_partner(sent_half.astype(jnp.bfloat16), 'seq', bit_index...  7.18 us
  transfers between devices with their start and end apart: 8, of which 7 were waited for; matrix products, arithmetic and copies ran while one was open for 3% of the time, Pallas kernels for 0%

commit v1 on v0

--- a/solution.py
+++ b/solution.py
@@ -1,6 +1,10 @@
+import functools
+
 import jax
 import jax.numpy as jnp
 from jax import lax
+from jax.experimental import pallas as pl
+from jax.experimental.pallas import tpu as pltpu
 from jax.sharding import PartitionSpec as P
 
 WIN = 256
@@ -139,9 +143,439 @@
     return (input_grad, buffer)
 
 
+BF = jnp.bfloat16
+F32 = jnp.float32
+NZ = 4
+ORDER = (0, 1, 3, 2)
+
+
+def dot_nn(a, b):
+    return jnp.dot(a, b, preferred_element_type=F32)
+
+
+def dot_nt(a, b):
+    return lax.dot_general(a, b, (((1,), (1,)), ((), ())), preferred_element_type=F32)
+
+
+def dot_tn(a, b):
+    return lax.dot_general(a, b, (((0,), (0,)), ((), ())), preferred_element_type=F32)
+
+
+def flip(v, f):
+    return v + f * (1 - 2 * v)
+
+
+def remote(src, dst, send, recv, device):
+    return pltpu.make_async_remote_copy(
+        src_ref=src,
+        dst_ref=dst,
+        send_sem=send,
+        recv_sem=recv,
+        device_id=device,
+        device_id_type=pl.DeviceIdType.MESH,
+    )
+
+
+def fused(
+    x_hbm, doc_ref, w_hbm, do_ref, dx_hbm, g_ref,
+    xv, xt, wv, acc, qs, dos, kv, dkv, pst, dst_, gp, dxv,
+    gb, rd, sb, rb, sa, ra, sz, rz, kz,
+    lsem, wsend, wrecv, hsend, hrecv, gsend, grecv, osem,
+):
+    s = lax.axis_index("seq")
+    d = lax.axis_index("dp")
+    z, y = s // 2, s % 2
+    x, c = d // 2, d % 2
+    tok = xv.shape[0]
+    rows = wv.shape[1]
+    hd = qs.shape[1]
+    inv_root = hd ** (-0.5)
+    my_a = x * (1 - c) + y * c
+    my_b = y * (1 - c) + x * c
+
+    def device(zz, yy, xx, cc):
+        return (zz * 2 + yy, xx * 2 + cc)
+
+    sib = device(z, y, x, 1 - c)
+    part_a = device(z, flip(y, c), flip(x, 1 - c), c)
+    part_b = device(z, flip(y, 1 - c), flip(x, c), c)
+    zdev = [device((z + k) % NZ, y, x, c) for k in range(NZ)]
+
+    def plane_block(k, a, b, plane):
+        zz = (z + NZ - k) % NZ
+        xx = flip(x, a * (1 - plane) + b * plane)
+        yy = flip(y, b * (1 - plane) + a * plane)
+        return ((zz * 2 + yy) * 2 + xx) * 2 + plane
+
+    load_w = pltpu.make_async_copy(w_hbm, wv.at[s * 4 + d], lsem.at[0])
+    load_x = pltpu.make_async_copy(x_hbm.at[0], xv, lsem.at[1])
+    load_w.start()
+    load_x.start()
+
+    barrier = pltpu.get_barrier_semaphore()
+    for dev in [sib, part_a, part_b] + zdev[1:]:
+        pl.semaphore_signal(barrier, inc=1, device_id=dev, device_id_type=pl.DeviceIdType.MESH)
+    extra_up = (y == 1) & (z < NZ - 1)
+    extra_down = (y == 0) & (z > 0)
+
+    @pl.when(extra_up)
+    def _():
+        pl.semaphore_signal(
+            barrier, inc=1, device_id=(s + 1, d), device_id_type=pl.DeviceIdType.MESH
+        )
+
+    @pl.when(extra_down)
+    def _():
+        pl.semaphore_signal(
+            barrier, inc=1, device_id=(s - 1, d), device_id_type=pl.DeviceIdType.MESH
+        )
+
+    @pl.when(extra_up | extra_down)
+    def _():
+        pl.semaphore_wait(barrier, 7)
+
+    @pl.when(jnp.logical_not(extra_up | extra_down))
+    def _():
+        pl.semaphore_wait(barrier, 6)
+
+    load_w.wait()
+
+    sent = []
+
+    def push(block, dev, send_index, recv_index):
+        copy = remote(
+            wv.at[block], wv.at[block], wsend.at[send_index], wrecv.at[recv_index], dev
+        )
+        copy.start()
+        sent.append(copy)
+
+    def arrived(block, index):
+        remote(wv.at[block], wv.at[block], wsend.at[0], wrecv.at[index], sib).wait_recv()
+
+    own = plane_block(0, 0, 0, c)
+
+    def stage_z(k):
+        block = plane_block(k, 0, 0, c)
+        if k:
+            arrived(block, k)
+        push(block, part_a, 4 + k, 4 + k)
+        push(block, part_b, 8 + 2 * k, 8 + 2 * k)
+        if k == 0:
+            for j in ORDER[1:]:
+                push(own, zdev[j], j, j)
+        push(block, sib, 16 + 4 * k, 16 + 4 * k)
+
+    def stage_a(k):
+        block = plane_block(k, 1, 0, c)
+        arrived(block, 4 + k)
+        push(block, part_b, 9 + 2 * k, 9 + 2 * k)
+        push(block, sib, 17 + 4 * k, 17 + 4 * k)
+
+    def stage_b(k):
+        for a in range(2):
+            block = plane_block(k, a, 1, c)
+            arrived(block, 8 + 2 * k + a)
+            push(block, sib, 18 + 4 * k + a, 18 + 4 * k + a)
+
+    def stage_d(k):
+        for b in range(2):
+            for a in range(2):
+                arrived(plane_block(k, a, b, 1 - c), 16 + 4 * k + 2 * b + a)
+        zz = (z + NZ - k) % NZ
+        span = 8 * rows
+        xs = xv[:, pl.ds(pl.multiple_of(zz * span, span), span)]
+        ws = wv[pl.ds(zz * 8, 8)].reshape(span, wv.shape[2])
+        part = dot_nn(xs, ws)
+        if k == ORDER[0]:
+            acc[...] = part
+        else:
+            acc[...] += part
+
+    def transpose_x(j, carry):
+        zz, yy, xx, cc = j // 8, (j // 4) % 2, (j // 2) % 2, j % 2
+        b_at = yy * (1 - cc) + xx * cc
+        a_at = xx * (1 - cc) + yy * cc
+        xt[cc, b_at, a_at, zz] = xv[:, pl.ds(pl.multiple_of(j * rows, rows), rows)].T
+        return carry
+
+    for t in range(NZ + 3):
+        if t < NZ:
+            stage_z(ORDER[t])
+        if t == 0:
+            load_x.wait()
+            doc = jnp.broadcast_to(doc_ref[...], (tok, tok)).T
+        if 0 <= t - 1 < NZ:
+            stage_a(ORDER[t - 1])
+        if 0 <= t - 2 < NZ:
+            stage_b(ORDER[t - 2])
+        if 0 <= t - 3 < NZ:
+            stage_d(ORDER[t - 3])
+        if t < NZ:
+            lax.fori_loop(t * 8, t * 8 + 8, transpose_x, 0)
+        if t == 1:
+            row = lax.broadcasted_iota(jnp.int32, (tok, tok), 0)
+            col = lax.broadcasted_iota(jnp.int32, (tok, tok), 1)
+            vis_own = jnp.where((col <= row) & (col + s * tok >= doc), 0.0, -jnp.inf)
+            vis_pri = jnp.where((col > row) & (col + (s - 1) * tok >= doc), 0.0, -jnp.inf)
+            for h in range(2):
+                dos[h * tok : (h + 1) * tok, :] = do_ref[0, :, h * hd : (h + 1) * hd]
+
+    kv[1] = acc[:, 2 * hd :].astype(BF)
+    halo = remote(kv.at[1], kv.at[0], hsend.at[0], hrecv.at[0], ((s + 1) % 8, d))
+    first, last = s == 0, s == 7
+
+    @pl.when(s < 7)
+    def _():
+        halo.start()
+
+    @pl.when(first)
+    def _():
+        kv[0] = jnp.zeros_like(kv[0])
+
+    for h in range(2):
+        qs[h * tok : (h + 1) * tok, :] = acc[:, h * hd : (h + 1) * hd].astype(BF)
+    k_own = kv[1, :, :hd]
+    v_own = kv[1, :, hd:]
+    own_scores = [
+        dot_nt(qs[h * tok : (h + 1) * tok, :], k_own) * inv_root + vis_own for h in range(2)
+    ]
+    own_pg = [dot_nt(dos[h * tok : (h + 1) * tok, :], v_own) for h in range(2)]
+
+    @pl.when(s > 0)
+    def _():
+        halo.wait_recv()
+
+    k_pri = kv[0, :, :hd]
+    v_pri = kv[0, :, hd:]
+    for h in range(2):
+        span = slice(h * tok, (h + 1) * tok)
+        s_own = own_scores[h]
+        s_pri = dot_nt(qs[span, :], k_pri) * inv_root + vis_pri
+        pg_own = own_pg[h]
+        pg_pri = dot_nt(dos[span, :], v_pri)
+        top = jnp.max(jnp.maximum(s_own, s_pri), axis=1, keepdims=True)
+        e_own = jnp.exp(s_own - top)
+        e_pri = jnp.exp(s_pri - top)
+        scale = 1.0 / jnp.sum(e_own + e_pri, axis=1, keepdims=True)
+        p_own = e_own * scale
+        p_pri = e_pri * scale
+        l_own = p_own.astype(BF)
+        l_pri = p_pri.astype(BF)
+        row_dot = jnp.sum(
+            l_own.astype(F32) * pg_own + l_pri.astype(F32) * pg_pri, axis=1, keepdims=True
+        )
+        pst[0, span, :] = l_pri
+        pst[1, span, :] = l_own
+        dst_[0, span, :] = (p_pri * (pg_pri - row_dot)).astype(BF)
+        dst_[1, span, :] = (p_own * (pg_own - row_dot)).astype(BF)
+
+    dkv[0, :, :hd] = (dot_tn(dst_[0], qs[...]) * inv_root).astype(BF)
+    dkv[0, :, hd:] = dot_tn(pst[0], dos[...]).astype(BF)
+    back = remote(dkv.at[0], dkv.at[1], hsend.at[1], hrecv.at[1], ((s + 7) % 8, d))
+
+    @pl.when(s > 0)
+    def _():
+        back.start()
+
+    @pl.when(last)
+    def _():
+        dkv[1] = jnp.zeros_like(dkv[1])
+
+    for h in range(2):
+        span = slice(h * tok, (h + 1) * tok)
+        gp[:, h * hd : (h + 1) * hd] = (
+            (dot_nn(dst_[1, span, :], k_own) + dot_nn(dst_[0, span, :], k_pri)) * inv_root
+        ).astype(BF)
+
+    half = 2 * hd
+    rsent = []
+
+    def weight_part(h, plane, b_at):
+        gph = gp[:, h * half : (h + 1) * half]
+
+        def one(j, carry):
+            a_at, zz = j // 2, (j % 2) * 2
+            lhs = xt[plane, b_at, a_at, pl.ds(zz, 2)].reshape(2 * rows, tok)
+            gb[h, plane, b_at, a_at, pl.ds(zz, 2)] = (
+                dot_nn(lhs, gph).astype(BF).reshape(2, rows, half)
+            )
+            return carry
+
+        lax.fori_loop(0, 4, one, 0)
+
+    def rpush(src, dst, index, dev):
+        copy = remote(src, dst, gsend.at[index], grecv.at[index], dev)
+        copy.start()
+        rsent.append(copy)
+        return copy
+
+    def produce(h):
+        copies = []
+        for j in range(2):
+            b_at = flip(my_a, 1 - j)
+            weight_part(h, 1 - c, b_at)
+            copies.append(rpush(gb.at[h, 1 - c, b_at], rd.at[h, j], 7 * h + j, sib))
+        weight_part(h, c, 1 - my_b)
+        weight_part(h, c, my_b)
+        return copies
+
+    def send_b(h, copies):
+        copies[0].wait_recv()
+
+        def one(j, carry):
+            a_at, zz = j // NZ, j % NZ
+            sb[h, a_at, zz] = (
+                gb[h, c, 1 - my_b, a_at, zz].astype(F32) + rd[h, 0, a_at, zz].astype(F32)
+            ).astype(BF)
+            return carry
+
+        lax.fori_loop(0, 2 * NZ, one, 0)
+        return rpush(sb.at[h], rb.at[h], 7 * h + 2, part_b)
+
+    def sum_b(h, a_at, zz):
+        return (
+            gb[h, c, my_b, a_at, zz].astype(F32)
+            + rd[h, 1, a_at, zz].astype(F32)
+            + rb[h, a_at, zz].astype(F32)
+        )
+
+    def send_a(h, copies, copy_b):
+        copies[1].wait_recv()
+        copy_b.wait_recv()
+
+        def one(zz, carry):
+            sa[h, zz] = sum_b(h, 1 - my_a, zz).astype(BF)
+            return carry
+
+        lax.fori_loop(0, NZ, one, 0)
+        return rpush(sa.at[h], ra.at[h], 7 * h + 3, part_a)
+
+    def send_z(h, copy_a):
+        copy_a.wait_recv()
+        copies = []
+        for k in (2, 1, 3):
+            zz = (z + k) % NZ
+            sz[h, k] = (sum_b(h, my_a, zz) + ra[h, zz].astype(F32)).astype(BF)
+            copies.append(rpush(sz.at[h, k], rz.at[h, k], 7 * h + 3 + k, zdev[k]))
+        kz[h] = sum_b(h, my_a, z) + ra[h, z].astype(F32)
+        return copies
+
+    def finish(h, copies):
+        for copy in copies:
+            copy.wait_recv()
+        g_ref[:, h * half : (h + 1) * half] = (
+            kz[h] + rz[h, 1].astype(F32) + rz[h, 2].astype(F32) + rz[h, 3].astype(F32)
+        )
+
+    d0 = produce(0)
+    own_dk = dot_tn(dst_[1], qs[...]) * inv_root
+    own_dv = dot_tn(pst[1], dos[...])
+    b0 = send_b(0, d0)
+
+    @pl.when(s < 7)
+    def _():
+        back.wait_recv()
+
+    gp[:, half : half + hd] = (own_dk + dkv[1, :, :hd].astype(F32)).astype(BF)
+    gp[:, half + hd :] = (own_dv + dkv[1, :, hd:].astype(F32)).astype(BF)
+    d1 = produce(1)
+    b1 = send_b(1, d1)
+
+    def input_grad(j, carry):
+        width = dxv.shape[1] // 8
+        at = pl.multiple_of(j * width, width)
+        ws = wv[pl.ds(j * 4, 4)].reshape(width, wv.shape[2])
+        dxv[:, pl.ds(at, width)] = dot_nt(gp[...], ws).astype(BF)
+        return carry
+
+    lax.fori_loop(0, 8, input_grad, 0)
+    store_dx = pltpu.make_async_copy(dxv, dx_hbm.at[0], osem)
+    store_dx.start()
+
+    a0 = send_a(0, d0, b0)
+    z0 = send_z(0, a0)
+    a1 = send_a(1, d1, b1)
+    z1 = send_z(1, a1)
+    finish(0, z0)
+    finish(1, z1)
+
+    store_dx.wait()
+    for copy in sent + rsent:
+        copy.wait_send()
+
+    @pl.when(s < 7)
+    def _():
+        halo.wait_send()
+
+    @pl.when(s > 0)
+    def _():
+        back.wait_send()
+
+
+def kernel_body(layer_inputs, doc_start, w_qkv, d_context):
+    tok, width = layer_inputs.shape[1:]
+    rows, cols = w_qkv.shape
+    hd = cols // 4
+    half = 2 * hd
+    blocks = width // rows
+    dma = pltpu.SemaphoreType.DMA
+    return pl.pallas_call(
+        fused,
+        out_shape=(
+            jax.ShapeDtypeStruct(layer_inputs.shape, BF),
+            jax.ShapeDtypeStruct((rows, cols), F32),
+        ),
+        in_specs=[
+            pl.BlockSpec(memory_space=pl.ANY),
+            pl.BlockSpec(memory_space=pltpu.VMEM),
+            pl.BlockSpec(memory_space=pl.ANY),
+            pl.BlockSpec(memory_space=pltpu.VMEM),
+        ],
+        out_specs=(
+            pl.BlockSpec(memory_space=pl.ANY),
+            pl.BlockSpec(memory_space=pltpu.VMEM),
+        ),
+        scratch_shapes=[
+            pltpu.VMEM((tok, width), BF),
+            pltpu.VMEM((2, 2, 2, NZ, rows, tok), BF),
+            pltpu.VMEM((blocks, rows, cols), BF),
+            pltpu.VMEM((tok, cols), F32),
+            pltpu.VMEM((2 * tok, hd), BF),
+            pltpu.VMEM((2 * tok, hd), BF),
+            pltpu.VMEM((2, tok, half), BF),
+            pltpu.VMEM((2, tok, half), BF),
+            pltpu.VMEM((2, 2 * tok, tok), BF),
+            pltpu.VMEM((2, 2 * tok, tok), BF),
+            pltpu.VMEM((tok, cols), BF),
+            pltpu.VMEM((tok, width), BF),
+            pltpu.VMEM((2, 2, 2, 2, NZ, rows, half), BF),
+            pltpu.VMEM((2, 2, 2, NZ, rows, half), BF),
+            pltpu.VMEM((2, 2, NZ, rows, half), BF),
+            pltpu.VMEM((2, 2, NZ, rows, half), BF),
+            pltpu.VMEM((2, NZ, rows, half), BF),
+            pltpu.VMEM((2, NZ, rows, half), BF),
+            pltpu.VMEM((2, NZ, rows, half), BF),
+            pltpu.VMEM((2, NZ, rows, half), BF),
+            pltpu.VMEM((2, rows, half), F32),
+            dma((2,)),
+            dma((32,)),
+            dma((32,)),
+            dma((2,)),
+            dma((2,)),
+            dma((14,)),
+            dma((14,)),
+            dma,
+        ],
+        compiler_params=pltpu.CompilerParams(
+            collective_id=0, has_side_effects=True, vmem_limit_bytes=48 * 1024 * 1024
+        ),
+    )(layer_inputs, doc_start, w_qkv, d_context)
+
+
 def solution(mesh):
+    fits = mesh.shape["seq"] == 8 and mesh.shape["dp"] == 4
     return jax.shard_map(
-        body,
+        kernel_body if fits else body,
         mesh=mesh,
         in_specs=(
             P("dp", "seq", None),

time: 265 us -> 76.7 us (0.29)
  waiting for transfers between devices: 204 us -> 0 us
  Pallas kernels: 0 us -> 69.7 us
  starting transfers between devices: 14 us -> 0 us
  between operations: 14.3 us -> 0.65 us
  matrix products: 11.3 us -> 0 us
  other arithmetic: 9.38 us -> 0 us
  local copies, waits for them, and re-layouts: 11.1 us -> 6.09 us
    ppermute x7 -> x0, waiting for transfers between devices: 138 us -> none  [the longest x5 129 us: from_partner(): return lax.ppermute(block, axis, route)]
    pallas_call x0 -> x1, Pallas kernels: none -> 69.7 us  [kernel_body(): pl.pallas_call(fused, out_shape=(jax.ShapeDtypeStruct(layer_inputs.shape,...]
    all_gather x1 -> x0, waiting for transfers between devices: 65.8 us -> none  [body(): full_weights = lax.all_gather(w_qkv, ('seq', 'dp'), axis=0, tiled=True)]
    ppermute x7 -> x0, starting transfers between devices: 13.9 us -> none  [the longest x5 9.27 us: from_partner(): return lax.ppermute(block, axis, route)]
    dot_general x9 -> x0, matrix products: 11.3 us -> none  [the longest x1 4.82 us: body(): lax.dot_general(grad_proj, full_weights, (((1,), (1,)), ((), ())), prefer...]
    add x7 -> x0, other arithmetic: 8.25 us -> none  [the longest x3 7.18 us: halve_over_seq(): kept_half + from_partner(sent_half.astype(jnp.bfloat16), 'seq', bit_index...]
  transfers between devices with their start and end apart: 8 -> 0, of which waited for: 7 -> 0; matrix products, arithmetic and copies ran while one was open for 3% -> 0% of each run, Pallas kernels for 0% -> 0%
where the time goes in v1:
time: 76.7 us; the launch traced here: 76.5 us
  Pallas kernels  69.7 us (91%)
  local copies, waits for them, and re-layouts  6.09 us (8%)
    pallas_call x1, Pallas kernels, kernel_body(): pl.pallas_call(fused, out_shape=(jax.ShapeDtypeStruct(layer_inputs.shape,...  69.7 us
    unnamed x10, local copies, waits for them, and re-layouts  6.09 us

profile of v1, /device:TPU:0, one launch (start us, length us, event | category | flops | bytes accessed | tf_op | source)
XLA Modules:
  0.0 76.5 jit_solution(17102898679565873736)
XLA Ops:
  0.6 0.0 copy-start
  0.6 1.6 %copy-done = bf16[1,256,4096]{2,1,0:T(8,128)(2,1)S(1)} copy-done((bf16[1,256,4096]{2,1,0:T(8,128)(2,1)S(1)}, bf16[1,256,4096]{2,1,0:T(8,128)(2,1)}, u32[]{:S(2)}) %copy-start) | copy-done | bytes 2097176
  2.2 0.0 copy-start.1
  2.2 0.9 %copy-done.1 = bf16[128,512]{1,0:T(8,128)(2,1)S(1)} copy-done((bf16[128,512]{1,0:T(8,128)(2,1)S(1)}, bf16[128,512]{1,0:T(8,128)(2,1)}, u32[]{:S(2)}) %copy-start.1) | copy-done | bytes 131096
  3.1 0.0 copy-start.2
  3.1 0.9 %copy-done.2 = bf16[1,256,256]{2,1,0:T(8,128)(2,1)S(1)} copy-done((bf16[1,256,256]{2,1,0:T(8,128)(2,1)S(1)}, bf16[1,256,256]{2,1,0:T(8,128)(2,1)}, u32[]{:S(2)}) %copy-start.2) | copy-done | bytes 131096
  4.0 0.0 copy-start.3
  4.0 0.7 copy-done.3
  4.7 69.7 %shard_map.59 = (bf16[1,256,4096]{2,1,0:T(8,128)(2,1)S(1)}, f32[128,512]{1,0:T(8,128)S(1)}) custom-call(bf16[1,256,4096]{2,1,0:T(8,128)(2,1)S(1)} %copy-done, s32[1,256]{1,0:T(1,128)S(1)} %copy-done.3, bf16[128,512]{1,0:T(8,128)(2,1)S(1)} %copy-done.1, bf16[1,256,256]{2,1,0:T(8,128)(2,1)S(1)} %copy-done.2), custom_call_target="tpu_custom_call" | custom-call | tf_op jit(solution)/shard_map/pallas_call | solution.py:522
  74.5 1.3 %copy.8 = bf16[1,256,4096]{2,1,0:T(8,128)(2,1)} copy(bf16[1,256,4096]{2,1,0:T(8,128)(2,1)S(1)} %get-tuple-element.4) | data formatting | bytes 4194304
  75.8 0.7 copy.9
Async XLA Ops:
  0.6 1.6 %copy-start = (bf16[1,256,4096]{2,1,0:T(8,128)(2,1)S(1)}, bf16[1,256,4096]{2,1,0:T(8,128)(2,1)}, u32[]{:S(2)}) copy-start(bf16[1,256,4096]{2,1,0:T(8,128)(2,1)} %x_hbm.1) | copy-start | bytes 6291460
  2.2 0.9 %copy-start.1 = (bf16[128,512]{1,0:T(8,128)(2,1)S(1)}, bf16[128,512]{1,0:T(8,128)(2,1)}, u32[]{:S(2)}) copy-start(bf16[128,512]{1,0:T(8,128)(2,1)} %w_hbm.1) | copy-start | bytes 393220
  3.1 0.9 %copy-start.2 = (bf16[1,256,256]{2,1,0:T(8,128)(2,1)S(1)}, bf16[1,256,256]{2,1,0:T(8,128)(2,1)}, u32[]{:S(2)}) copy-start(bf16[1,256,256]{2,1,0:T(8,128)(2,1)} %do_ref.1) | copy-start | bytes 393220
  4.0 0.7 copy-start.3

commit v2 on v1

--- a/solution.py
+++ b/solution.py
@@ -1,5 +1,3 @@
-import functools
-
 import jax
 import jax.numpy as jnp
 from jax import lax
@@ -176,9 +174,12 @@
     )
 
 
+CHUNKS = (2, 1, 3, 0)
+
+
 def fused(
-    x_hbm, doc_ref, w_hbm, do_ref, dx_hbm, g_ref,
-    xv, xt, wv, acc, qs, dos, kv, dkv, pst, dst_, gp, dxv,
+    x_hbm, doc_hbm, w_hbm, do_hbm, dx_hbm, g_ref,
+    xv, docv, xt, wv, acc, qs, dos, pgs, kv, dkv, pst, dst_, gp, dxv,
     gb, rd, sb, rb, sa, ra, sz, rz, kz,
     lsem, wsend, wrecv, hsend, hrecv, gsend, grecv, osem,
 ):
@@ -187,8 +188,9 @@
     z, y = s // 2, s % 2
     x, c = d // 2, d % 2
     tok = xv.shape[0]
-    rows = wv.shape[1]
+    rows = wv.shape[2]
     hd = qs.shape[1]
+    half = 2 * hd
     inv_root = hd ** (-0.5)
     my_a = x * (1 - c) + y * c
     my_b = y * (1 - c) + x * c
@@ -207,10 +209,20 @@
         yy = flip(y, b * (1 - plane) + a * plane)
         return ((zz * 2 + yy) * 2 + xx) * 2 + plane
 
-    load_w = pltpu.make_async_copy(w_hbm, wv.at[s * 4 + d], lsem.at[0])
-    load_x = pltpu.make_async_copy(x_hbm.at[0], xv, lsem.at[1])
-    load_w.start()
-    load_x.start()
+    own = s * 4 + d
+    loads = [
+        pltpu.make_async_copy(w_hbm.at[:, pl.ds(half, half)], wv.at[1, own], lsem.at[0]),
+        pltpu.make_async_copy(w_hbm.at[:, pl.ds(0, half)], wv.at[0, own], lsem.at[1]),
+        pltpu.make_async_copy(x_hbm.at[0], xv, lsem.at[2]),
+        pltpu.make_async_copy(doc_hbm, docv, lsem.at[3]),
+    ] + [
+        pltpu.make_async_copy(
+            do_hbm.at[0, :, pl.ds(h * hd, hd)], dos.at[pl.ds(h * tok, tok)], lsem.at[4 + h]
+        )
+        for h in range(2)
+    ]
+    for load in loads:
+        load.start()
 
     barrier = pltpu.get_barrier_semaphore()
     for dev in [sib, part_a, part_b] + zdev[1:]:
@@ -230,6 +242,9 @@
             barrier, inc=1, device_id=(s - 1, d), device_id_type=pl.DeviceIdType.MESH
         )
 
+    loads[0].wait()
+    loads[1].wait()
+
     @pl.when(extra_up | extra_down)
     def _():
         pl.semaphore_wait(barrier, 7)
@@ -238,121 +253,123 @@
     def _():
         pl.semaphore_wait(barrier, 6)
 
-    load_w.wait()
-
     sent = []
 
-    def push(block, dev, send_index, recv_index):
+    def push(h, block, dev, index):
         copy = remote(
-            wv.at[block], wv.at[block], wsend.at[send_index], wrecv.at[recv_index], dev
+            wv.at[h, block], wv.at[h, block], wsend.at[h, index], wrecv.at[h, index], dev
         )
         copy.start()
         sent.append(copy)
 
-    def arrived(block, index):
-        remote(wv.at[block], wv.at[block], wsend.at[0], wrecv.at[index], sib).wait_recv()
-
-    own = plane_block(0, 0, 0, c)
-
-    def stage_z(k):
+    def arrived(h, block, index):
+        ref = wv.at[h, block]
+        remote(ref, ref, wsend.at[h, 0], wrecv.at[h, index], sib).wait_recv()
+
+    def push_z(h):
+        for k in ORDER[1:]:
+            push(h, own, zdev[k], k)
+
+    def stage_z(h, k):
         block = plane_block(k, 0, 0, c)
         if k:
-            arrived(block, k)
-        push(block, part_a, 4 + k, 4 + k)
-        push(block, part_b, 8 + 2 * k, 8 + 2 * k)
-        if k == 0:
-            for j in ORDER[1:]:
-                push(own, zdev[j], j, j)
-        push(block, sib, 16 + 4 * k, 16 + 4 * k)
-
-    def stage_a(k):
+            arrived(h, block, k)
+        push(h, block, part_a, 4 + k)
+        push(h, block, part_b, 8 + 2 * k)
+        push(h, block, sib, 16 + 4 * k)
+
+    def stage_a(h, k):
         block = plane_block(k, 1, 0, c)
-        arrived(block, 4 + k)
-        push(block, part_b, 9 + 2 * k, 9 + 2 * k)
-        push(block, sib, 17 + 4 * k, 17 + 4 * k)
-
-    def stage_b(k):
+        arrived(h, block, 4 + k)
+        push(h, block, part_b, 9 + 2 * k)
+        push(h, block, sib, 17 + 4 * k)
+
+    def stage_b(h, k):
         for a in range(2):
             block = plane_block(k, a, 1, c)
-            arrived(block, 8 + 2 * k + a)
-            push(block, sib, 18 + 4 * k + a, 18 + 4 * k + a)
-
-    def stage_d(k):
+            arrived(h, block, 8 + 2 * k + a)
+            push(h, block, sib, 18 + 4 * k + a)
+
+    def stage_d(h, k):
         for b in range(2):
             for a in range(2):
-                arrived(plane_block(k, a, b, 1 - c), 16 + 4 * k + 2 * b + a)
+                arrived(h, plane_block(k, a, b, 1 - c), 16 + 4 * k + 2 * b + a)
         zz = (z + NZ - k) % NZ
         span = 8 * rows
         xs = xv[:, pl.ds(pl.multiple_of(zz * span, span), span)]
-        ws = wv[pl.ds(zz * 8, 8)].reshape(span, wv.shape[2])
-        part = dot_nn(xs, ws)
+        part = dot_nn(xs, wv[h, pl.ds(zz * 8, 8)].reshape(span, half))
         if k == ORDER[0]:
-            acc[...] = part
+            acc[h] = part
         else:
-            acc[...] += part
+            acc[h] += part
 
     def transpose_x(j, carry):
         zz, yy, xx, cc = j // 8, (j // 4) % 2, (j // 2) % 2, j % 2
         b_at = yy * (1 - cc) + xx * cc
         a_at = xx * (1 - cc) + yy * cc
-        xt[cc, b_at, a_at, zz] = xv[:, pl.ds(pl.multiple_of(j * rows, rows), rows)].T
+        xt[zz, cc, b_at, a_at] = xv[:, pl.ds(pl.multiple_of(j * rows, rows), rows)].T
         return carry
 
-    for t in range(NZ + 3):
-        if t < NZ:
-            stage_z(ORDER[t])
+    halo = remote(kv.at[1], kv.at[0], hsend.at[0], hrecv.at[0], ((s + 1) % 8, d))
+
+    def send_halo():
+        kv[1] = acc[1].astype(BF)
+
+        @pl.when(s < 7)
+        def _():
+            halo.start()
+
+        @pl.when(s == 0)
+        def _():
+            kv[0] = jnp.zeros_like(kv[0])
+
+    def value_grads():
+        @pl.when(s > 0)
+        def _():
+            halo.wait_recv()
+
+        for j in range(2):
+            pgs[j] = dot_nt(dos[...], kv[j, :, hd:])
+
+    steps = [(h, k) for h in (1, 0) for k in ORDER]
+    n_steps = len(steps)
+    push_z(1)
+    for t in range(n_steps + 3):
+        if t == 3:
+            push_z(0)
+        if 0 <= t - 1 < n_steps:
+            stage_a(*steps[t - 1])
+        if t < n_steps:
+            stage_z(*steps[t])
+        if 0 <= t - 2 < n_steps:
+            stage_b(*steps[t - 2])
         if t == 0:
-            load_x.wait()
-            doc = jnp.broadcast_to(doc_ref[...], (tok, tok)).T
-        if 0 <= t - 1 < NZ:
-            stage_a(ORDER[t - 1])
-        if 0 <= t - 2 < NZ:
-            stage_b(ORDER[t - 2])
-        if 0 <= t - 3 < NZ:
-            stage_d(ORDER[t - 3])
-        if t < NZ:
-            lax.fori_loop(t * 8, t * 8 + 8, transpose_x, 0)
-        if t == 1:
+            for load in loads[2:]:
+                load.wait()
+            doc = jnp.broadcast_to(docv[...], (tok, tok)).T
             row = lax.broadcasted_iota(jnp.int32, (tok, tok), 0)
             col = lax.broadcasted_iota(jnp.int32, (tok, tok), 1)
             vis_own = jnp.where((col <= row) & (col + s * tok >= doc), 0.0, -jnp.inf)
             vis_pri = jnp.where((col > row) & (col + (s - 1) * tok >= doc), 0.0, -jnp.inf)
-            for h in range(2):
-                dos[h * tok : (h + 1) * tok, :] = do_ref[0, :, h * hd : (h + 1) * hd]
-
-    kv[1] = acc[:, 2 * hd :].astype(BF)
-    halo = remote(kv.at[1], kv.at[0], hsend.at[0], hrecv.at[0], ((s + 1) % 8, d))
-    first, last = s == 0, s == 7
-
-    @pl.when(s < 7)
-    def _():
-        halo.start()
-
-    @pl.when(first)
-    def _():
-        kv[0] = jnp.zeros_like(kv[0])
+        if t == n_steps + 2:
+            value_grads()
+        if 0 <= t - 3 < n_steps:
+            stage_d(*steps[t - 3])
+        if t == 6:
+            send_halo()
+        if t < n_steps:
+            lax.fori_loop(t * 4, t * 4 + 4, transpose_x, 0)
 
     for h in range(2):
-        qs[h * tok : (h + 1) * tok, :] = acc[:, h * hd : (h + 1) * hd].astype(BF)
+        qs[h * tok : (h + 1) * tok, :] = acc[0, :, h * hd : (h + 1) * hd].astype(BF)
     k_own = kv[1, :, :hd]
-    v_own = kv[1, :, hd:]
-    own_scores = [
-        dot_nt(qs[h * tok : (h + 1) * tok, :], k_own) * inv_root + vis_own for h in range(2)
-    ]
-    own_pg = [dot_nt(dos[h * tok : (h + 1) * tok, :], v_own) for h in range(2)]
-
-    @pl.when(s > 0)
-    def _():
-        halo.wait_recv()
-
     k_pri = kv[0, :, :hd]
-    v_pri = kv[0, :, hd:]
     for h in range(2):
         span = slice(h * tok, (h + 1) * tok)
-        s_own = own_scores[h]
+        s_own = dot_nt(qs[span, :], k_own) * inv_root + vis_own
         s_pri = dot_nt(qs[span, :], k_pri) * inv_root + vis_pri
-        pg_own = own_pg[h]
-        pg_pri = dot_nt(dos[span, :], v_pri)
+        pg_own = pgs[1, span, :]
+        pg_pri = pgs[0, span, :]
         top = jnp.max(jnp.maximum(s_own, s_pri), axis=1, keepdims=True)
         e_own = jnp.exp(s_own - top)
         e_pri = jnp.exp(s_pri - top)
@@ -377,130 +394,111 @@
     def _():
         back.start()
 
-    @pl.when(last)
+    @pl.when(s == 7)
     def _():
         dkv[1] = jnp.zeros_like(dkv[1])
 
     for h in range(2):
         span = slice(h * tok, (h + 1) * tok)
-        gp[:, h * hd : (h + 1) * hd] = (
+        gp[0, :, h * hd : (h + 1) * hd] = (
             (dot_nn(dst_[1, span, :], k_own) + dot_nn(dst_[0, span, :], k_pri)) * inv_root
         ).astype(BF)
 
-    half = 2 * hd
-    rsent = []
-
-    def weight_part(h, plane, b_at):
-        gph = gp[:, h * half : (h + 1) * half]
-
-        def one(j, carry):
-            a_at, zz = j // 2, (j % 2) * 2
-            lhs = xt[plane, b_at, a_at, pl.ds(zz, 2)].reshape(2 * rows, tok)
-            gb[h, plane, b_at, a_at, pl.ds(zz, 2)] = (
-                dot_nn(lhs, gph).astype(BF).reshape(2, rows, half)
-            )
-            return carry
-
-        lax.fori_loop(0, 4, one, 0)
-
-    def rpush(src, dst, index, dev):
+    rsent = {}
+
+    def rpush(src, dst, h, k, stage, dev):
+        index = (h * NZ + k) * 4 + stage
         copy = remote(src, dst, gsend.at[index], grecv.at[index], dev)
         copy.start()
-        rsent.append(copy)
-        return copy
-
-    def produce(h):
-        copies = []
-        for j in range(2):
-            b_at = flip(my_a, 1 - j)
-            weight_part(h, 1 - c, b_at)
-            copies.append(rpush(gb.at[h, 1 - c, b_at], rd.at[h, j], 7 * h + j, sib))
-        weight_part(h, c, 1 - my_b)
-        weight_part(h, c, my_b)
-        return copies
-
-    def send_b(h, copies):
-        copies[0].wait_recv()
-
-        def one(j, carry):
-            a_at, zz = j // NZ, j % NZ
-            sb[h, a_at, zz] = (
-                gb[h, c, 1 - my_b, a_at, zz].astype(F32) + rd[h, 0, a_at, zz].astype(F32)
-            ).astype(BF)
-            return carry
-
-        lax.fori_loop(0, 2 * NZ, one, 0)
-        return rpush(sb.at[h], rb.at[h], 7 * h + 2, part_b)
-
-    def sum_b(h, a_at, zz):
-        return (
-            gb[h, c, my_b, a_at, zz].astype(F32)
-            + rd[h, 1, a_at, zz].astype(F32)
-            + rb[h, a_at, zz].astype(F32)
+        rsent[h, k, stage] = copy
+
+    def weight_part(h, k, plane):
+        lhs = xt[(z + k) % NZ, plane].reshape(4 * rows, tok)
+        gb[h, k, plane] = dot_nn(lhs, gp[h]).astype(BF).reshape(2, 2, rows, half)
+
+    def produce(h, k):
+        weight_part(h, k, 1 - c)
+        rpush(gb.at[h, k, 1 - c], rd.at[h, k], h, k, 0, sib)
+        weight_part(h, k, c)
+
+    def chip_sum(h, k, b_at, a_at):
+        return gb[h, k, c, b_at, a_at].astype(F32) + rd[h, k, b_at, a_at].astype(F32)
+
+    def send_b(h, k):
+        rsent[h, k, 0].wait_recv()
+        for a_at in range(2):
+            sb[h, k, a_at] = chip_sum(h, k, 1 - my_b, a_at).astype(BF)
+        rpush(sb.at[h, k], rb.at[h, k], h, k, 1, part_b)
+
+    def send_a(h, k):
+        rsent[h, k, 1].wait_recv()
+        sa[h, k] = (
+            chip_sum(h, k, my_b, 1 - my_a) + rb[h, k, 1 - my_a].astype(F32)
+        ).astype(BF)
+        rpush(sa.at[h, k], ra.at[h, k], h, k, 2, part_a)
+
+    def send_z(h, k):
+        rsent[h, k, 2].wait_recv()
+        total = (
+            chip_sum(h, k, my_b, my_a)
+            + rb[h, k, my_a].astype(F32)
+            + ra[h, k].astype(F32)
         )
-
-    def send_a(h, copies, copy_b):
-        copies[1].wait_recv()
-        copy_b.wait_recv()
-
-        def one(zz, carry):
-            sa[h, zz] = sum_b(h, 1 - my_a, zz).astype(BF)
-            return carry
-
-        lax.fori_loop(0, NZ, one, 0)
-        return rpush(sa.at[h], ra.at[h], 7 * h + 3, part_a)
-
-    def send_z(h, copy_a):
-        copy_a.wait_recv()
-        copies = []
-        for k in (2, 1, 3):
-            zz = (z + k) % NZ
-            sz[h, k] = (sum_b(h, my_a, zz) + ra[h, zz].astype(F32)).astype(BF)
-            copies.append(rpush(sz.at[h, k], rz.at[h, k], 7 * h + 3 + k, zdev[k]))
-        kz[h] = sum_b(h, my_a, z) + ra[h, z].astype(F32)
-        return copies
-
-    def finish(h, copies):
-        for copy in copies:
-            copy.wait_recv()
-        g_ref[:, h * half : (h + 1) * half] = (
-            kz[h] + rz[h, 1].astype(F32) + rz[h, 2].astype(F32) + rz[h, 3].astype(F32)
-        )
-
-    d0 = produce(0)
-    own_dk = dot_tn(dst_[1], qs[...]) * inv_root
-    own_dv = dot_tn(pst[1], dos[...])
-    b0 = send_b(0, d0)
-
-    @pl.when(s < 7)
-    def _():
-        back.wait_recv()
-
-    gp[:, half : half + hd] = (own_dk + dkv[1, :, :hd].astype(F32)).astype(BF)
-    gp[:, half + hd :] = (own_dv + dkv[1, :, hd:].astype(F32)).astype(BF)
-    d1 = produce(1)
-    b1 = send_b(1, d1)
+        if k:
+            sz[h, k] = total.astype(BF)
+            rpush(sz.at[h, k], rz.at[h, k], h, k, 3, zdev[k])
+        else:
+            kz[h] = total
+
+    def finish(h):
+        total = kz[h]
+        for k in CHUNKS[:3]:
+            rsent[h, k, 3].wait_recv()
+            total += rz[h, k].astype(F32)
+        g_ref[:, h * half : (h + 1) * half] = total
 
     def input_grad(j, carry):
         width = dxv.shape[1] // 8
         at = pl.multiple_of(j * width, width)
-        ws = wv[pl.ds(j * 4, 4)].reshape(width, wv.shape[2])
-        dxv[:, pl.ds(at, width)] = dot_nt(gp[...], ws).astype(BF)
+        ws = [wv[h, pl.ds(j * 4, 4)].reshape(width, half) for h in range(2)]
+        dxv[:, pl.ds(at, width)] = (dot_nt(gp[0], ws[0]) + dot_nt(gp[1], ws[1])).astype(BF)
         return carry
 
-    lax.fori_loop(0, 8, input_grad, 0)
+    for i in range(NZ + 1):
+        if i < NZ:
+            produce(0, CHUNKS[i])
+        if i > 0:
+            send_b(0, CHUNKS[i - 1])
+    own_dk = dot_tn(dst_[1], qs[...]) * inv_root
+    own_dv = dot_tn(pst[1], dos[...])
+
+    @pl.when(s < 7)
+    def _():
+        back.wait_recv()
+
+    gp[1, :, :hd] = (own_dk + dkv[1, :, :hd].astype(F32)).astype(BF)
+    gp[1, :, hd:] = (own_dv + dkv[1, :, hd:].astype(F32)).astype(BF)
+    for i in range(NZ + 1):
+        if i < NZ:
+            produce(1, CHUNKS[i])
+            send_a(0, CHUNKS[i])
+        if i > 0:
+            send_b(1, CHUNKS[i - 1])
+    for i in range(NZ):
+        send_z(0, CHUNKS[i])
+        lax.fori_loop(2 * i, 2 * i + 2, input_grad, 0)
     store_dx = pltpu.make_async_copy(dxv, dx_hbm.at[0], osem)
     store_dx.start()
-
-    a0 = send_a(0, d0, b0)
-    z0 = send_z(0, a0)
-    a1 = send_a(1, d1, b1)
-    z1 = send_z(1, a1)
-    finish(0, z0)
-    finish(1, z1)
+    for i in range(NZ + 1):
+        if i < NZ:
+            send_a(1, CHUNKS[i])
+        if i > 0:
+            send_z(1, CHUNKS[i - 1])
+    finish(0)
+    finish(1)
 
     store_dx.wait()
-    for copy in sent + rsent:
+    for copy in sent + list(rsent.values()):
         copy.wait_send()
 
     @pl.when(s < 7)
@@ -519,55 +517,53 @@
     half = 2 * hd
     blocks = width // rows
     dma = pltpu.SemaphoreType.DMA
+    block = (rows, half)
     return pl.pallas_call(
         fused,
         out_shape=(
             jax.ShapeDtypeStruct(layer_inputs.shape, BF),
             jax.ShapeDtypeStruct((rows, cols), F32),
         ),
-        in_specs=[
-            pl.BlockSpec(memory_space=pl.ANY),
-            pl.BlockSpec(memory_space=pltpu.VMEM),
-            pl.BlockSpec(memory_space=pl.ANY),
-            pl.BlockSpec(memory_space=pltpu.VMEM),
-        ],
+        in_specs=[pl.BlockSpec(memory_space=pl.ANY)] * 4,
         out_specs=(
             pl.BlockSpec(memory_space=pl.ANY),
             pl.BlockSpec(memory_space=pltpu.VMEM),
         ),
         scratch_shapes=[
             pltpu.VMEM((tok, width), BF),
-            pltpu.VMEM((2, 2, 2, NZ, rows, tok), BF),
-            pltpu.VMEM((blocks, rows, cols), BF),
-            pltpu.VMEM((tok, cols), F32),
+            pltpu.VMEM((1, tok), jnp.int32),
+            pltpu.VMEM((NZ, 2, 2, 2, rows, tok), BF),
+            pltpu.VMEM((2, blocks) + block, BF),
+            pltpu.VMEM((2, tok, half), F32),
             pltpu.VMEM((2 * tok, hd), BF),
             pltpu.VMEM((2 * tok, hd), BF),
+            pltpu.VMEM((2, 2 * tok, tok), F32),
             pltpu.VMEM((2, tok, half), BF),
             pltpu.VMEM((2, tok, half), BF),
             pltpu.VMEM((2, 2 * tok, tok), BF),
             pltpu.VMEM((2, 2 * tok, tok), BF),
-            pltpu.VMEM((tok, cols), BF),
+            pltpu.VMEM((2, tok, half), BF),
             pltpu.VMEM((tok, width), BF),
-            pltpu.VMEM((2, 2, 2, 2, NZ, rows, half), BF),
-            pltpu.VMEM((2, 2, 2, NZ, rows, half), BF),
-            pltpu.VMEM((2, 2, NZ, rows, half), BF),
-            pltpu.VMEM((2, 2, NZ, rows, half), BF),
-            pltpu.VMEM((2, NZ, rows, half), BF),
-            pltpu.VMEM((2, NZ, rows, half), BF),
-            pltpu.VMEM((2, NZ, rows, half), BF),
-            pltpu.VMEM((2, NZ, rows, half), BF),
-            pltpu.VMEM((2, rows, half), F32),
+            pltpu.VMEM((2, NZ, 2, 2, 2) + block, BF),
+            pltpu.VMEM((2, NZ, 2, 2) + block, BF),
+            pltpu.VMEM((2, NZ, 2) + block, BF),
+            pltpu.VMEM((2, NZ, 2) + block, BF),
+            pltpu.VMEM((2, NZ) + block, BF),
+            pltpu.VMEM((2, NZ) + block, BF),
+            pltpu.VMEM((2, NZ) + block, BF),
+            pltpu.VMEM((2, NZ) + block, BF),
+            pltpu.VMEM((2,) + block, F32),
+            dma((6,)),
+            dma((2, 32)),
+            dma((2, 32)),
+            dma((2,)),
             dma((2,)),
             dma((32,)),
             dma((32,)),
-            dma((2,)),
-            dma((2,)),
-            dma((14,)),
-            dma((14,)),
             dma,
         ],
         compiler_params=pltpu.CompilerParams(
-            collective_id=0, has_side_effects=True, vmem_limit_bytes=48 * 1024 * 1024
+            collective_id=0, has_side_effects=True, vmem_limit_bytes=60 * 1024 * 1024
         ),
     )(layer_inputs, doc_start, w_qkv, d_context)
 

time: 76.7 us -> 74.1 us (0.966)
  local copies, waits for them, and re-layouts: 6.09 us -> 3.88 us
    unnamed x10 -> x4, local copies, waits for them, and re-layouts: 6.09 us -> 3.88 us
where the time goes in v2:
time: 74.1 us; the launch traced here: 74 us
  Pallas kernels  69.4 us (94%)
  local copies, waits for them, and re-layouts  3.88 us (5%)
    pallas_call x1, Pallas kernels, kernel_body(): pl.pallas_call(fused, out_shape=(jax.ShapeDtypeStruct(layer_inputs.shape,...  69.4 us
    unnamed x4, local copies, waits for them, and re-layouts  3.88 us

profile of v2, /device:TPU:0, one launch (start us, length us, event | category | flops | bytes accessed | tf_op | source)
XLA Modules:
  0.0 74.0 jit_solution(6894800584839706773)
XLA Ops:
  0.6 69.4 %shard_map.59 = (bf16[1,256,4096]{2,1,0:T(8,128)(2,1)}, f32[128,512]{1,0:T(8,128)}) custom-call(bf16[1,256,4096]{2,1,0:T(8,128)(2,1)} %x_hbm.1, s32[1,256]{1,0:T(1,128)} %doc_hbm.1, bf16[128,512]{1,0:T(8,128)(2,1)} %w_hbm.1, bf16[1,256,256]{2,1,0:T(8,128)(2,1)} %do_hbm.1), custom_call_target="tpu_custom_call" | custom-call | tf_op jit(solution)/shard_map/pallas_call | solution.py:521
  70.1 0.0 copy-start
  70.1 3.2 %copy.8 = bf16[1,256,4096]{2,1,0:T(8,128)(2,1)} copy(bf16[1,256,4096]{2,1,0:T(8,128)(2,1)} %get-tuple-element.4) | data formatting | bytes 4194304
  73.3 0.0 copy-done
  73.3 0.7 copy.9
Async XLA Ops:
  70.1 3.2 %copy-start = (f32[128,512]{1,0:T(8,128)S(1)}, f32[128,512]{1,0:T(8,128)}, u32[]{:S(2)}) copy-start(f32[128,512]{1,0:T(8,128)} %get-tuple-element.5) | copy-start | bytes 786436

commit v3 on v2

--- a/solution.py
+++ b/solution.py
@@ -144,7 +144,16 @@
 BF = jnp.bfloat16
 F32 = jnp.float32
 NZ = 4
-ORDER = (0, 1, 3, 2)
+ORDER = (
+    ("z", 1, 0), ("z", 1, 1), ("a", 1, 0), ("b", 1, 0, 0), ("z", 1, 2), ("prep",), ("a", 1, 1),
+    ("b", 1, 1, 0), ("b", 1, 0, 1), ("z", 1, 3), ("turn", 0), ("b", 1, 2, 0), ("a", 1, 2),
+    ("turn", 1), ("b", 1, 1, 1), ("b", 1, 3, 0), ("a", 1, 3), ("z", 0, 0), ("d", 1, 0),
+    ("b", 1, 2, 1), ("d", 1, 1), ("z", 0, 1), ("b", 1, 3, 1), ("z", 0, 2), ("a", 0, 0),
+    ("d", 1, 2), ("b", 0, 0, 0), ("d", 1, 3), ("halo",), ("z", 0, 3), ("b", 0, 1, 0),
+    ("b", 0, 2, 0), ("a", 0, 1), ("a", 0, 2), ("turn", 2), ("b", 0, 0, 1), ("turn", 3),
+    ("b", 0, 2, 1), ("a", 0, 3), ("b", 0, 3, 0), ("b", 0, 1, 1), ("d", 0, 0), ("values",),
+    ("b", 0, 3, 1), ("d", 0, 1), ("d", 0, 2), ("d", 0, 3),
+)
 
 
 def dot_nn(a, b):
@@ -203,8 +212,15 @@
     part_b = device(z, flip(y, 1 - c), flip(x, c), c)
     zdev = [device((z + k) % NZ, y, x, c) for k in range(NZ)]
 
+    z_order = [
+        z,
+        jnp.where(z == 0, 1, jnp.where(z == 1, 0, jnp.where(z == 2, 3, 2))),
+        jnp.where(z == 0, 2, jnp.where(z == 1, 2, 1)),
+        jnp.where(z <= 1, 3, 0),
+    ]
+
     def plane_block(k, a, b, plane):
-        zz = (z + NZ - k) % NZ
+        zz = z_order[k]
         xx = flip(x, a * (1 - plane) + b * plane)
         yy = flip(y, b * (1 - plane) + a * plane)
         return ((zz * 2 + yy) * 2 + xx) * 2 + plane
@@ -266,14 +282,24 @@
         ref = wv.at[h, block]
         remote(ref, ref, wsend.at[h, 0], wrecv.at[h, index], sib).wait_recv()
 
-    def push_z(h):
-        for k in ORDER[1:]:
-            push(h, own, zdev[k], k)
+    line = []
+
+    def push_line(h, block, zz):
+        up = remote(
+            wv.at[h, block], wv.at[h, block], wsend.at[h, zz], wrecv.at[h, zz], zdev[1]
+        )
+        down = remote(
+            wv.at[h, block], wv.at[h, block], wsend.at[h, 32 + zz], wrecv.at[h, zz], zdev[3]
+        )
+        for copy, test in ((up, (zz <= z) & (z < NZ - 1)), (down, (zz >= z) & (z > 0))):
+            line.append((copy, test))
+            pl.when(test)(copy.start)
 
     def stage_z(h, k):
         block = plane_block(k, 0, 0, c)
         if k:
-            arrived(h, block, k)
+            arrived(h, block, z_order[k])
+        push_line(h, block, z_order[k])
         push(h, block, part_a, 4 + k)
         push(h, block, part_b, 8 + 2 * k)
         push(h, block, sib, 16 + 4 * k)
@@ -284,21 +310,20 @@
         push(h, block, part_b, 9 + 2 * k)
         push(h, block, sib, 17 + 4 * k)
 
-    def stage_b(h, k):
-        for a in range(2):
-            block = plane_block(k, a, 1, c)
-            arrived(h, block, 8 + 2 * k + a)
-            push(h, block, sib, 18 + 4 * k + a)
+    def stage_b(h, k, a):
+        block = plane_block(k, a, 1, c)
+        arrived(h, block, 8 + 2 * k + a)
+        push(h, block, sib, 18 + 4 * k + a)
 
     def stage_d(h, k):
         for b in range(2):
             for a in range(2):
                 arrived(h, plane_block(k, a, b, 1 - c), 16 + 4 * k + 2 * b + a)
-        zz = (z + NZ - k) % NZ
+        zz = z_order[k]
         span = 8 * rows
         xs = xv[:, pl.ds(pl.multiple_of(zz * span, span), span)]
         part = dot_nn(xs, wv[h, pl.ds(zz * 8, 8)].reshape(span, half))
-        if k == ORDER[0]:
+        if k == 0:
             acc[h] = part
         else:
             acc[h] += part
@@ -331,19 +356,22 @@
         for j in range(2):
             pgs[j] = dot_nt(dos[...], kv[j, :, hd:])
 
-    steps = [(h, k) for h in (1, 0) for k in ORDER]
-    n_steps = len(steps)
-    push_z(1)
-    for t in range(n_steps + 3):
-        if t == 3:
-            push_z(0)
-        if 0 <= t - 1 < n_steps:
-            stage_a(*steps[t - 1])
-        if t < n_steps:
-            stage_z(*steps[t])
-        if 0 <= t - 2 < n_steps:
-            stage_b(*steps[t - 2])
-        if t == 0:
+    for stage, *at in ORDER:
+        if stage == "z":
+            stage_z(*at)
+        elif stage == "a":
+            stage_a(*at)
+        elif stage == "b":
+            stage_b(*at)
+        elif stage == "d":
+            stage_d(*at)
+        elif stage == "turn":
+            lax.fori_loop(at[0] * 8, at[0] * 8 + 8, transpose_x, 0)
+        elif stage == "halo":
+            send_halo()
+        elif stage == "values":
+            value_grads()
+        else:
             for load in loads[2:]:
                 load.wait()
             doc = jnp.broadcast_to(docv[...], (tok, tok)).T
@@ -351,14 +379,6 @@
             col = lax.broadcasted_iota(jnp.int32, (tok, tok), 1)
             vis_own = jnp.where((col <= row) & (col + s * tok >= doc), 0.0, -jnp.inf)
             vis_pri = jnp.where((col > row) & (col + (s - 1) * tok >= doc), 0.0, -jnp.inf)
-        if t == n_steps + 2:
-            value_grads()
-        if 0 <= t - 3 < n_steps:
-            stage_d(*steps[t - 3])
-        if t == 6:
-            send_halo()
-        if t < n_steps:
-            lax.fori_loop(t * 4, t * 4 + 4, transpose_x, 0)
 
     for h in range(2):
         qs[h * tok : (h + 1) * tok, :] = acc[0, :, h * hd : (h + 1) * hd].astype(BF)
@@ -464,13 +484,17 @@
         dxv[:, pl.ds(at, width)] = (dot_nt(gp[0], ws[0]) + dot_nt(gp[1], ws[1])).astype(BF)
         return carry
 
-    for i in range(NZ + 1):
-        if i < NZ:
-            produce(0, CHUNKS[i])
-        if i > 0:
-            send_b(0, CHUNKS[i - 1])
+    c0, c1, c2, c3 = CHUNKS
+    produce(0, c0)
+    produce(0, c1)
+    produce(0, c2)
+    send_b(0, c0)
+    produce(0, c3)
+    send_b(0, c1)
+    send_b(0, c2)
     own_dk = dot_tn(dst_[1], qs[...]) * inv_root
     own_dv = dot_tn(pst[1], dos[...])
+    send_b(0, c3)
 
     @pl.when(s < 7)
     def _():
@@ -478,28 +502,46 @@
 
     gp[1, :, :hd] = (own_dk + dkv[1, :, :hd].astype(F32)).astype(BF)
     gp[1, :, hd:] = (own_dv + dkv[1, :, hd:].astype(F32)).astype(BF)
-    for i in range(NZ + 1):
-        if i < NZ:
-            produce(1, CHUNKS[i])
-            send_a(0, CHUNKS[i])
-        if i > 0:
-            send_b(1, CHUNKS[i - 1])
-    for i in range(NZ):
-        send_z(0, CHUNKS[i])
-        lax.fori_loop(2 * i, 2 * i + 2, input_grad, 0)
+    def grads(lo, hi):
+        lax.fori_loop(lo, hi, input_grad, 0)
+
+    produce(1, c0)
+    send_a(0, c0)
+    produce(1, c1)
+    send_b(1, c0)
+    send_a(0, c1)
+    produce(1, c2)
+    send_b(1, c1)
+    send_z(0, c0)
+    send_a(0, c2)
+    produce(1, c3)
+    send_b(1, c2)
+    send_z(0, c1)
+    send_a(0, c3)
+    send_b(1, c3)
+    grads(0, 3)
+    send_z(0, c2)
+    send_a(1, c0)
+    grads(3, 6)
+    send_z(0, c3)
+    send_a(1, c1)
+    send_z(1, c0)
+    grads(6, 8)
     store_dx = pltpu.make_async_copy(dxv, dx_hbm.at[0], osem)
     store_dx.start()
-    for i in range(NZ + 1):
-        if i < NZ:
-            send_a(1, CHUNKS[i])
-        if i > 0:
-            send_z(1, CHUNKS[i - 1])
+    send_a(1, c2)
+    send_z(1, c1)
+    send_a(1, c3)
+    send_z(1, c2)
+    send_z(1, c3)
     finish(0)
     finish(1)
 
     store_dx.wait()
     for copy in sent + list(rsent.values()):
         copy.wait_send()
+    for copy, test in line:
+        pl.when(test)(copy.wait_send)
 
     @pl.when(s < 7)
     def _():
@@ -554,7 +596,7 @@
             pltpu.VMEM((2, NZ) + block, BF),
             pltpu.VMEM((2,) + block, F32),
             dma((6,)),
-            dma((2, 32)),
+            dma((2, 36)),
             dma((2, 32)),
             dma((2,)),
             dma((2,)),

time: 74.1 us -> 73.6 us (level)
  no operation moved by 1% of the time
where the time goes in v3:
time: 73.6 us; the launch traced here: 73.4 us
  Pallas kernels  68.9 us (94%)
  local copies, waits for them, and re-layouts  3.88 us (5%)
    pallas_call x1, Pallas kernels, kernel_body(): pl.pallas_call(fused, out_shape=(jax.ShapeDtypeStruct(layer_inputs.shape,...  68.9 us
    unnamed x4, local copies, waits for them, and re-layouts  3.88 us

profile of v3, /device:TPU:0, one launch (start us, length us, event | category | flops | bytes accessed | tf_op | source)
XLA Modules:
  0.0 73.4 jit_solution(10620242958685682154)
XLA Ops:
  0.6 68.9 %shard_map.59 = (bf16[1,256,4096]{2,1,0:T(8,128)(2,1)}, f32[128,512]{1,0:T(8,128)}) custom-call(bf16[1,256,4096]{2,1,0:T(8,128)(2,1)} %x_hbm.1, s32[1,256]{1,0:T(1,128)} %doc_hbm.1, bf16[128,512]{1,0:T(8,128)(2,1)} %w_hbm.1, bf16[1,256,256]{2,1,0:T(8,128)(2,1)} %do_hbm.1), custom_call_target="tpu_custom_call" | custom-call | tf_op jit(solution)/shard_map/pallas_call | solution.py:563
  69.5 0.0 copy-start
  69.5 3.2 %copy.8 = bf16[1,256,4096]{2,1,0:T(8,128)(2,1)} copy(bf16[1,256,4096]{2,1,0:T(8,128)(2,1)} %get-tuple-element.4) | data formatting | bytes 4194304
  72.7 0.0 copy-done
  72.7 0.7 copy.9
Async XLA Ops:
  69.5 3.2 %copy-start = (f32[128,512]{1,0:T(8,128)S(1)}, f32[128,512]{1,0:T(8,128)}, u32[]{:S(2)}) copy-start(f32[128,512]{1,0:T(8,128)} %get-tuple-element.5) | copy-start | bytes 786436

commit v4 on v3

--- a/solution.py
+++ b/solution.py
@@ -145,15 +145,16 @@
 F32 = jnp.float32
 NZ = 4
 ORDER = (
-    ("z", 1, 0), ("z", 1, 1), ("a", 1, 0), ("b", 1, 0, 0), ("z", 1, 2), ("prep",), ("a", 1, 1),
-    ("b", 1, 1, 0), ("b", 1, 0, 1), ("z", 1, 3), ("turn", 0), ("b", 1, 2, 0), ("a", 1, 2),
-    ("turn", 1), ("b", 1, 1, 1), ("b", 1, 3, 0), ("a", 1, 3), ("z", 0, 0), ("d", 1, 0),
-    ("b", 1, 2, 1), ("d", 1, 1), ("z", 0, 1), ("b", 1, 3, 1), ("z", 0, 2), ("a", 0, 0),
-    ("d", 1, 2), ("b", 0, 0, 0), ("d", 1, 3), ("halo",), ("z", 0, 3), ("b", 0, 1, 0),
-    ("b", 0, 2, 0), ("a", 0, 1), ("a", 0, 2), ("turn", 2), ("b", 0, 0, 1), ("turn", 3),
-    ("b", 0, 2, 1), ("a", 0, 3), ("b", 0, 3, 0), ("b", 0, 1, 1), ("d", 0, 0), ("values",),
-    ("b", 0, 3, 1), ("d", 0, 1), ("d", 0, 2), ("d", 0, 3),
+    ("z", 1, 0), ("swap",), ("z", 1, 1), ("a", 1, 0), ("b", 1, 0, 0), ("z", 1, 2), ("a", 1, 1),
+    ("b", 1, 1, 0), ("b", 1, 0, 1), ("z", 1, 3), ("prep",), ("b", 1, 2, 0), ("a", 1, 2),
+    ("b", 1, 1, 1), ("b", 1, 3, 0), ("a", 1, 3), ("z", 0, 0), ("take",), ("d", 1, 0),
+    ("b", 1, 2, 1), ("d", 1, 1), ("z", 0, 1), ("b", 1, 3, 1), ("d", 1, 2), ("z", 0, 2),
+    ("d", 1, 3), ("partial", 1), ("a", 0, 0), ("b", 0, 0, 0), ("halo",), ("z", 0, 3),
+    ("b", 0, 1, 0), ("b", 0, 2, 0), ("a", 0, 1), ("a", 0, 2), ("b", 0, 0, 1), ("d", 0, 0),
+    ("b", 0, 2, 1), ("a", 0, 3), ("b", 0, 3, 0), ("b", 0, 1, 1), ("d", 0, 1), ("d", 0, 2),
+    ("values",), ("b", 0, 3, 1), ("d", 0, 3), ("partial", 0),
 )
+CHUNKS = (2, 1, 3, 0)
 
 
 def dot_nn(a, b):
@@ -183,23 +184,21 @@
     )
 
 
-CHUNKS = (2, 1, 3, 0)
-
-
 def fused(
     x_hbm, doc_hbm, w_hbm, do_hbm, dx_hbm, g_ref,
-    xv, docv, xt, wv, acc, qs, dos, pgs, kv, dkv, pst, dst_, gp, dxv,
-    gb, rd, sb, rb, sa, ra, sz, rz, kz,
-    lsem, wsend, wrecv, hsend, hrecv, gsend, grecv, osem,
+    xo, xs, docv, wv, acc, pacc, qs, qt, dos, dot_, pgs, kv, dkv, pst, dst_, gp, gpt, dxo, dxr,
+    gb, rb, sa, ra, sz, rz, kz,
+    lsem, xsem, wsend, wrecv, hsend, hrecv, ssend, srecv, gsend, grecv, osem,
 ):
     s = lax.axis_index("seq")
     d = lax.axis_index("dp")
     z, y = s // 2, s % 2
     x, c = d // 2, d % 2
-    tok = xv.shape[0]
-    rows = wv.shape[2]
+    tok = xs.shape[1]
+    rows = wv.shape[4]
     hd = qs.shape[1]
     half = 2 * hd
+    span = 4 * rows
     inv_root = hd ** (-0.5)
     my_a = x * (1 - c) + y * c
     my_b = y * (1 - c) + x * c
@@ -211,7 +210,6 @@
     part_a = device(z, flip(y, c), flip(x, 1 - c), c)
     part_b = device(z, flip(y, 1 - c), flip(x, c), c)
     zdev = [device((z + k) % NZ, y, x, c) for k in range(NZ)]
-
     z_order = [
         z,
         jnp.where(z == 0, 1, jnp.where(z == 1, 0, jnp.where(z == 2, 3, 2))),
@@ -219,25 +217,53 @@
         jnp.where(z <= 1, 3, 0),
     ]
 
-    def plane_block(k, a, b, plane):
-        zz = z_order[k]
-        xx = flip(x, a * (1 - plane) + b * plane)
-        yy = flip(y, b * (1 - plane) + a * plane)
-        return ((zz * 2 + yy) * 2 + xx) * 2 + plane
-
-    own = s * 4 + d
+    def columns(plane, zz, q):
+        b, a = q // 2, q % 2
+        yy = b * (1 - plane) + a * plane
+        xx = a * (1 - plane) + b * plane
+        block = ((zz * 2 + yy) * 2 + xx) * 2 + plane
+        return pl.ds(pl.multiple_of(block * rows, rows), rows)
+
+    def load_swap(j):
+        zz, q = j // 4, j % 4
+        return pltpu.make_async_copy(
+            x_hbm.at[0, :, columns(1 - c, zz, q)],
+            xs.at[zz, :, pl.ds(pl.multiple_of(q * rows, rows), rows)],
+            xsem.at[j],
+        )
+
+    def load_own(j):
+        zz, q = j // 4, j % 4
+        return pltpu.make_async_copy(
+            x_hbm.at[0, :, columns(c, zz, q)],
+            xo.at[zz, pl.ds(0, tok), pl.ds(pl.multiple_of(q * rows, rows), rows)],
+            xsem.at[16 + j],
+        )
+
+    def each(count, action):
+        def one(j, carry):
+            action(j)
+            return carry
+
+        lax.fori_loop(0, count, one, 0)
+
     loads = [
-        pltpu.make_async_copy(w_hbm.at[:, pl.ds(half, half)], wv.at[1, own], lsem.at[0]),
-        pltpu.make_async_copy(w_hbm.at[:, pl.ds(0, half)], wv.at[0, own], lsem.at[1]),
-        pltpu.make_async_copy(x_hbm.at[0], xv, lsem.at[2]),
-        pltpu.make_async_copy(doc_hbm, docv, lsem.at[3]),
-    ] + [
         pltpu.make_async_copy(
-            do_hbm.at[0, :, pl.ds(h * hd, hd)], dos.at[pl.ds(h * tok, tok)], lsem.at[4 + h]
+            w_hbm.at[:, pl.ds(h * half, half)], wv.at[h, z, my_b, my_a], lsem.at[h]
+        )
+        for h in (1, 0)
+    ]
+    late = [pltpu.make_async_copy(doc_hbm, docv, lsem.at[2])] + [
+        pltpu.make_async_copy(
+            do_hbm.at[0, :, pl.ds(h * hd, hd)], dos.at[pl.ds(h * tok, tok)], lsem.at[3 + h]
         )
         for h in range(2)
     ]
     for load in loads:
+        load.start()
+    each(16, lambda j: load_swap(j).start())
+    each(16, lambda j: load_own(j).start())
+    for load in late:
         load.start()
 
     barrier = pltpu.get_barrier_semaphore()
@@ -270,75 +296,63 @@
         pl.semaphore_wait(barrier, 6)
 
     sent = []
-
-    def push(h, block, dev, index):
-        copy = remote(
-            wv.at[h, block], wv.at[h, block], wsend.at[h, index], wrecv.at[h, index], dev
-        )
+    line = []
+    swaps = {}
+
+    def swap(src, dst, index):
+        copy = remote(src, dst, ssend.at[index], srecv.at[index], sib)
         copy.start()
         sent.append(copy)
-
-    def arrived(h, block, index):
-        ref = wv.at[h, block]
+        swaps[index] = copy
+
+    def block_at(h, k, b_flip, a_flip):
+        return wv.at[h, z_order[k], flip(my_b, b_flip), flip(my_a, a_flip)]
+
+    def push(h, ref, dev, index):
+        copy = remote(ref, ref, wsend.at[h, index], wrecv.at[h, index], dev)
+        copy.start()
+        sent.append(copy)
+
+    def arrived(h, ref, index):
         remote(ref, ref, wsend.at[h, 0], wrecv.at[h, index], sib).wait_recv()
 
-    line = []
-
-    def push_line(h, block, zz):
-        up = remote(
-            wv.at[h, block], wv.at[h, block], wsend.at[h, zz], wrecv.at[h, zz], zdev[1]
-        )
-        down = remote(
-            wv.at[h, block], wv.at[h, block], wsend.at[h, 32 + zz], wrecv.at[h, zz], zdev[3]
-        )
+    def stage_z(h, k):
+        ref = block_at(h, k, 0, 0)
+        zz = z_order[k]
+        if k:
+            arrived(h, ref, zz)
+        up = remote(ref, ref, wsend.at[h, zz], wrecv.at[h, zz], zdev[1])
+        down = remote(ref, ref, wsend.at[h, 16 + zz], wrecv.at[h, zz], zdev[3])
         for copy, test in ((up, (zz <= z) & (z < NZ - 1)), (down, (zz >= z) & (z > 0))):
             line.append((copy, test))
             pl.when(test)(copy.start)
-
-    def stage_z(h, k):
-        block = plane_block(k, 0, 0, c)
-        if k:
-            arrived(h, block, z_order[k])
-        push_line(h, block, z_order[k])
-        push(h, block, part_a, 4 + k)
-        push(h, block, part_b, 8 + 2 * k)
-        push(h, block, sib, 16 + 4 * k)
+        push(h, ref, part_a, 4 + k)
+        push(h, ref, part_b, 8 + 2 * k)
 
     def stage_a(h, k):
-        block = plane_block(k, 1, 0, c)
-        arrived(h, block, 4 + k)
-        push(h, block, part_b, 9 + 2 * k)
-        push(h, block, sib, 17 + 4 * k)
+        ref = block_at(h, k, 0, 1)
+        arrived(h, ref, 4 + k)
+        push(h, ref, part_b, 9 + 2 * k)
 
     def stage_b(h, k, a):
-        block = plane_block(k, a, 1, c)
-        arrived(h, block, 8 + 2 * k + a)
-        push(h, block, sib, 18 + 4 * k + a)
+        arrived(h, block_at(h, k, 1, a), 8 + 2 * k + a)
 
     def stage_d(h, k):
-        for b in range(2):
-            for a in range(2):
-                arrived(h, plane_block(k, a, b, 1 - c), 16 + 4 * k + 2 * b + a)
         zz = z_order[k]
-        span = 8 * rows
-        xs = xv[:, pl.ds(pl.multiple_of(zz * span, span), span)]
-        part = dot_nn(xs, wv[h, pl.ds(zz * 8, 8)].reshape(span, half))
+        part = dot_nn(xo[zz], wv[h, zz].reshape(span, half))
         if k == 0:
             acc[h] = part
         else:
             acc[h] += part
 
-    def transpose_x(j, carry):
-        zz, yy, xx, cc = j // 8, (j // 4) % 2, (j // 2) % 2, j % 2
-        b_at = yy * (1 - cc) + xx * cc
-        a_at = xx * (1 - cc) + yy * cc
-        xt[zz, cc, b_at, a_at] = xv[:, pl.ds(pl.multiple_of(j * rows, rows), rows)].T
-        return carry
+    def projected(h):
+        swaps[4 + h].wait_recv()
+        return (acc[h, :tok] + pacc[h]).astype(BF)
 
     halo = remote(kv.at[1], kv.at[0], hsend.at[0], hrecv.at[0], ((s + 1) % 8, d))
 
     def send_halo():
-        kv[1] = acc[1].astype(BF)
+        kv[1] = projected(1)
 
         @pl.when(s < 7)
         def _():
@@ -365,31 +379,42 @@
             stage_b(*at)
         elif stage == "d":
             stage_d(*at)
-        elif stage == "turn":
-            lax.fori_loop(at[0] * 8, at[0] * 8 + 8, transpose_x, 0)
+        elif stage == "swap":
+            each(16, lambda j: load_swap(j).wait())
+            for j in range(NZ):
+                swap(xs.at[j], xo.at[j, pl.ds(tok, tok)], j)
+        elif stage == "take":
+            each(16, lambda j: load_own(j).wait())
+            for j in range(NZ):
+                swaps[j].wait_recv()
+        elif stage == "partial":
+            swap(acc.at[at[0], pl.ds(tok, tok)], pacc.at[at[0]], 4 + at[0])
         elif stage == "halo":
             send_halo()
         elif stage == "values":
             value_grads()
         else:
-            for load in loads[2:]:
+            for load in late:
                 load.wait()
             doc = jnp.broadcast_to(docv[...], (tok, tok)).T
             row = lax.broadcasted_iota(jnp.int32, (tok, tok), 0)
             col = lax.broadcasted_iota(jnp.int32, (tok, tok), 1)
             vis_own = jnp.where((col <= row) & (col + s * tok >= doc), 0.0, -jnp.inf)
             vis_pri = jnp.where((col > row) & (col + (s - 1) * tok >= doc), 0.0, -jnp.inf)
-
+            dot_[...] = dos[...].T
+
+    q_own = projected(0)
     for h in range(2):
-        qs[h * tok : (h + 1) * tok, :] = acc[0, :, h * hd : (h + 1) * hd].astype(BF)
+        qs[h * tok : (h + 1) * tok, :] = q_own[:, h * hd : (h + 1) * hd]
+    qt[...] = qs[...].T
     k_own = kv[1, :, :hd]
     k_pri = kv[0, :, :hd]
     for h in range(2):
-        span = slice(h * tok, (h + 1) * tok)
-        s_own = dot_nt(qs[span, :], k_own) * inv_root + vis_own
-        s_pri = dot_nt(qs[span, :], k_pri) * inv_root + vis_pri
-        pg_own = pgs[1, span, :]
-        pg_pri = pgs[0, span, :]
+        at = slice(h * tok, (h + 1) * tok)
+        s_own = dot_nt(qs[at, :], k_own) * inv_root + vis_own
+        s_pri = dot_nt(qs[at, :], k_pri) * inv_root + vis_pri
+        pg_own = pgs[1, at, :]
+        pg_pri = pgs[0, at, :]
         top = jnp.max(jnp.maximum(s_own, s_pri), axis=1, keepdims=True)
         e_own = jnp.exp(s_own - top)
         e_pri = jnp.exp(s_pri - top)
@@ -401,13 +426,13 @@
         row_dot = jnp.sum(
             l_own.astype(F32) * pg_own + l_pri.astype(F32) * pg_pri, axis=1, keepdims=True
         )
-        pst[0, span, :] = l_pri
-        pst[1, span, :] = l_own
-        dst_[0, span, :] = (p_pri * (pg_pri - row_dot)).astype(BF)
-        dst_[1, span, :] = (p_own * (pg_own - row_dot)).astype(BF)
-
-    dkv[0, :, :hd] = (dot_tn(dst_[0], qs[...]) * inv_root).astype(BF)
-    dkv[0, :, hd:] = dot_tn(pst[0], dos[...]).astype(BF)
+        pst[0, at, :] = l_pri
+        pst[1, at, :] = l_own
+        dst_[0, at, :] = (p_pri * (pg_pri - row_dot)).astype(BF)
+        dst_[1, at, :] = (p_own * (pg_own - row_dot)).astype(BF)
+
+    dkv[0, :hd, :] = (dot_nn(qt[...], dst_[0]) * inv_root).astype(BF)
+    dkv[0, hd:, :] = dot_nn(dot_[...], pst[0]).astype(BF)
     back = remote(dkv.at[0], dkv.at[1], hsend.at[1], hrecv.at[1], ((s + 7) % 8, d))
 
     @pl.when(s > 0)
@@ -419,125 +444,129 @@
         dkv[1] = jnp.zeros_like(dkv[1])
 
     for h in range(2):
-        span = slice(h * tok, (h + 1) * tok)
-        gp[0, :, h * hd : (h + 1) * hd] = (
-            (dot_nn(dst_[1, span, :], k_own) + dot_nn(dst_[0, span, :], k_pri)) * inv_root
+        at = slice(h * tok, (h + 1) * tok)
+        gp[0, :tok, h * hd : (h + 1) * hd] = (
+            (dot_nn(dst_[1, at, :], k_own) + dot_nn(dst_[0, at, :], k_pri)) * inv_root
         ).astype(BF)
 
     rsent = {}
 
+    def swap_grads(h):
+        swap(gp.at[h, pl.ds(0, tok)], gp.at[h, pl.ds(tok, tok)], 6 + h)
+
+    def take_grads(h):
+        swaps[6 + h].wait_recv()
+        gpt[h, :, tok:] = gp[h, tok:, :].T
+
     def rpush(src, dst, h, k, stage, dev):
-        index = (h * NZ + k) * 4 + stage
+        index = (h * NZ + k) * 3 + stage
         copy = remote(src, dst, gsend.at[index], grecv.at[index], dev)
         copy.start()
         rsent[h, k, stage] = copy
 
-    def weight_part(h, k, plane):
-        lhs = xt[(z + k) % NZ, plane].reshape(4 * rows, tok)
-        gb[h, k, plane] = dot_nn(lhs, gp[h]).astype(BF).reshape(2, 2, rows, half)
-
     def produce(h, k):
-        weight_part(h, k, 1 - c)
-        rpush(gb.at[h, k, 1 - c], rd.at[h, k], h, k, 0, sib)
-        weight_part(h, k, c)
-
-    def chip_sum(h, k, b_at, a_at):
-        return gb[h, k, c, b_at, a_at].astype(F32) + rd[h, k, b_at, a_at].astype(F32)
-
-    def send_b(h, k):
+        part = dot_nn(gpt[h], xo[(z + k) % NZ]).astype(BF)
+        for q in range(4):
+            gb[h, k, q // 2, q % 2] = part[:, q * rows : (q + 1) * rows]
+        rpush(gb.at[h, k, 1 - my_b], rb.at[h, k], h, k, 0, part_b)
+
+    def sum_b(h, k, a_at):
+        return gb[h, k, my_b, a_at].astype(F32) + rb[h, k, a_at].astype(F32)
+
+    def send_a(h, k):
         rsent[h, k, 0].wait_recv()
-        for a_at in range(2):
-            sb[h, k, a_at] = chip_sum(h, k, 1 - my_b, a_at).astype(BF)
-        rpush(sb.at[h, k], rb.at[h, k], h, k, 1, part_b)
-
-    def send_a(h, k):
+        sa[h, k] = sum_b(h, k, 1 - my_a).astype(BF)
+        rpush(sa.at[h, k], ra.at[h, k], h, k, 1, part_a)
+
+    def send_z(h, k):
         rsent[h, k, 1].wait_recv()
-        sa[h, k] = (
-            chip_sum(h, k, my_b, 1 - my_a) + rb[h, k, 1 - my_a].astype(F32)
-        ).astype(BF)
-        rpush(sa.at[h, k], ra.at[h, k], h, k, 2, part_a)
-
-    def send_z(h, k):
-        rsent[h, k, 2].wait_recv()
-        total = (
-            chip_sum(h, k, my_b, my_a)
-            + rb[h, k, my_a].astype(F32)
-            + ra[h, k].astype(F32)
-        )
+        total = sum_b(h, k, my_a) + ra[h, k].astype(F32)
         if k:
             sz[h, k] = total.astype(BF)
-            rpush(sz.at[h, k], rz.at[h, k], h, k, 3, zdev[k])
+            rpush(sz.at[h, k], rz.at[h, k], h, k, 2, zdev[k])
         else:
             kz[h] = total
 
     def finish(h):
         total = kz[h]
         for k in CHUNKS[:3]:
-            rsent[h, k, 3].wait_recv()
+            rsent[h, k, 2].wait_recv()
             total += rz[h, k].astype(F32)
-        g_ref[:, h * half : (h + 1) * half] = total
-
-    def input_grad(j, carry):
-        width = dxv.shape[1] // 8
-        at = pl.multiple_of(j * width, width)
-        ws = [wv[h, pl.ds(j * 4, 4)].reshape(width, half) for h in range(2)]
-        dxv[:, pl.ds(at, width)] = (dot_nt(gp[0], ws[0]) + dot_nt(gp[1], ws[1])).astype(BF)
-        return carry
+        g_ref[:, h * half : (h + 1) * half] = total.T
+
+    def store(src, plane, zz, q, index):
+        return pltpu.make_async_copy(
+            src.at[zz, pl.ds(0, tok), pl.ds(q * rows, rows)],
+            dx_hbm.at[0, :, columns(plane, zz, q)],
+            osem.at[index],
+        )
+
+    stores = []
+
+    def input_grad(zz):
+        part = dot_nt(gp[0], wv[0, zz].reshape(span, half))
+        part += dot_nt(gp[1], wv[1, zz].reshape(span, half))
+        dxo[zz] = part.astype(BF)
+        swap(dxo.at[zz, pl.ds(tok, tok)], dxr.at[zz], 8 + zz)
+        for q in range(4):
+            stores.append(store(dxo, c, zz, q, zz * 4 + q))
+            stores[-1].start()
+
+    def take_input_grad(zz):
+        swaps[8 + zz].wait_recv()
+        for q in range(4):
+            stores.append(store(dxr, 1 - c, zz, q, 16 + zz * 4 + q))
+            stores[-1].start()
 
     c0, c1, c2, c3 = CHUNKS
-    produce(0, c0)
-    produce(0, c1)
-    produce(0, c2)
-    send_b(0, c0)
-    produce(0, c3)
-    send_b(0, c1)
-    send_b(0, c2)
-    own_dk = dot_tn(dst_[1], qs[...]) * inv_root
-    own_dv = dot_tn(pst[1], dos[...])
-    send_b(0, c3)
+    swap_grads(0)
+    gpt[0, :, :tok] = gp[0, :tok, :].T
+    own_dk = dot_nn(qt[...], dst_[1]) * inv_root
+    own_dv = dot_nn(dot_[...], pst[1])
+    take_grads(0)
+    for k in CHUNKS:
+        produce(0, k)
 
     @pl.when(s < 7)
     def _():
         back.wait_recv()
 
-    gp[1, :, :hd] = (own_dk + dkv[1, :, :hd].astype(F32)).astype(BF)
-    gp[1, :, hd:] = (own_dv + dkv[1, :, hd:].astype(F32)).astype(BF)
-    def grads(lo, hi):
-        lax.fori_loop(lo, hi, input_grad, 0)
-
+    gpt[1, :hd, :tok] = (own_dk + dkv[1, :hd, :].astype(F32)).astype(BF)
+    gpt[1, hd:, :tok] = (own_dv + dkv[1, hd:, :].astype(F32)).astype(BF)
+    gp[1, :tok, :] = gpt[1, :, :tok].T
+    swap_grads(1)
+    send_a(0, c0)
+    take_grads(1)
     produce(1, c0)
-    send_a(0, c0)
+    send_a(0, c1)
     produce(1, c1)
-    send_b(1, c0)
-    send_a(0, c1)
-    produce(1, c2)
-    send_b(1, c1)
     send_z(0, c0)
     send_a(0, c2)
-    produce(1, c3)
-    send_b(1, c2)
+    produce(1, c2)
     send_z(0, c1)
     send_a(0, c3)
-    send_b(1, c3)
-    grads(0, 3)
+    produce(1, c3)
+    input_grad(0)
     send_z(0, c2)
+    input_grad(1)
     send_a(1, c0)
-    grads(3, 6)
     send_z(0, c3)
+    input_grad(2)
     send_a(1, c1)
     send_z(1, c0)
-    grads(6, 8)
-    store_dx = pltpu.make_async_copy(dxv, dx_hbm.at[0], osem)
-    store_dx.start()
+    input_grad(3)
+    for zz in range(NZ):
+        take_input_grad(zz)
     send_a(1, c2)
     send_z(1, c1)
+    finish(0)
     send_a(1, c3)
     send_z(1, c2)
     send_z(1, c3)
-    finish(0)
     finish(1)
 
-    store_dx.wait()
+    for copy in stores:
+        copy.wait()
     for copy in sent + list(rsent.values()):
         copy.wait_send()
     for copy, test in line:
@@ -557,9 +586,8 @@
     rows, cols = w_qkv.shape
     hd = cols // 4
     half = 2 * hd
-    blocks = width // rows
     dma = pltpu.SemaphoreType.DMA
-    block = (rows, half)
+    block = (half, rows)
     return pl.pallas_call(
         fused,
         out_shape=(
@@ -572,37 +600,43 @@
             pl.BlockSpec(memory_space=pltpu.VMEM),
         ),
         scratch_shapes=[
-            pltpu.VMEM((tok, width), BF),
+            pltpu.VMEM((NZ, 2 * tok, 4 * rows), BF),
+            pltpu.VMEM((NZ, tok, 4 * rows), BF),
             pltpu.VMEM((1, tok), jnp.int32),
-            pltpu.VMEM((NZ, 2, 2, 2, rows, tok), BF),
-            pltpu.VMEM((2, blocks) + block, BF),
+            pltpu.VMEM((2, NZ, 2, 2, rows, half), BF),
+            pltpu.VMEM((2, 2 * tok, half), F32),
             pltpu.VMEM((2, tok, half), F32),
             pltpu.VMEM((2 * tok, hd), BF),
+            pltpu.VMEM((hd, 2 * tok), BF),
             pltpu.VMEM((2 * tok, hd), BF),
+            pltpu.VMEM((hd, 2 * tok), BF),
             pltpu.VMEM((2, 2 * tok, tok), F32),
             pltpu.VMEM((2, tok, half), BF),
-            pltpu.VMEM((2, tok, half), BF),
+            pltpu.VMEM((2, half, tok), BF),
             pltpu.VMEM((2, 2 * tok, tok), BF),
             pltpu.VMEM((2, 2 * tok, tok), BF),
-            pltpu.VMEM((2, tok, half), BF),
-            pltpu.VMEM((tok, width), BF),
-            pltpu.VMEM((2, NZ, 2, 2, 2) + block, BF),
+            pltpu.VMEM((2, 2 * tok, half), BF),
+            pltpu.VMEM((2, half, 2 * tok), BF),
+            pltpu.VMEM((NZ, 2 * tok, 4 * rows), BF),
+            pltpu.VMEM((NZ, tok, 4 * rows), BF),
             pltpu.VMEM((2, NZ, 2, 2) + block, BF),
-            pltpu.VMEM((2, NZ, 2) + block, BF),
             pltpu.VMEM((2, NZ, 2) + block, BF),
             pltpu.VMEM((2, NZ) + block, BF),
             pltpu.VMEM((2, NZ) + block, BF),
             pltpu.VMEM((2, NZ) + block, BF),
             pltpu.VMEM((2, NZ) + block, BF),
             pltpu.VMEM((2,) + block, F32),
-            dma((6,)),
-            dma((2, 36)),
-            dma((2, 32)),
+            dma((5,)),
+            dma((32,)),
+            dma((2, 20)),
+            dma((2, 16)),
             dma((2,)),
             dma((2,)),
+            dma((12,)),
+            dma((12,)),
+            dma((24,)),
+            dma((24,)),
             dma((32,)),
-            dma((32,)),
-            dma,
         ],
         compiler_params=pltpu.CompilerParams(
             collective_id=0, has_side_effects=True, vmem_limit_bytes=60 * 1024 * 1024

time: 73.6 us -> 75.6 us (1.027)
  Pallas kernels: 68.9 us -> 70.9 us
    pallas_call x1, Pallas kernels: 68.9 us -> 70.9 us  [kernel_body(): pl.pallas_call(fused, out_shape=(jax.ShapeDtypeStruct(layer_inputs.shape,...]
where the time goes in v4:
time: 75.6 us; the launch traced here: 75.4 us
  Pallas kernels  70.9 us (94%)
  local copies, waits for them, and re-layouts  3.88 us (5%)
    pallas_call x1, Pallas kernels, kernel_body(): pl.pallas_call(fused, out_shape=(jax.ShapeDtypeStruct(layer_inputs.shape,...  70.9 us
    unnamed x4, local copies, waits for them, and re-layouts  3.88 us

profile of v4, /device:TPU:0, one launch (start us, length us, event | category | flops | bytes accessed | tf_op | source)
XLA Modules:
  0.0 75.4 jit_solution(17322147009968645905)
XLA Ops:
  0.6 70.9 %shard_map.59 = (bf16[1,256,4096]{2,1,0:T(8,128)(2,1)}, f32[128,512]{1,0:T(8,128)}) custom-call(bf16[1,256,4096]{2,1,0:T(8,128)(2,1)} %x_hbm.1, s32[1,256]{1,0:T(1,128)} %doc_hbm.1, bf16[128,512]{1,0:T(8,128)(2,1)} %w_hbm.1, bf16[1,256,256]{2,1,0:T(8,128)(2,1)} %do_hbm.1), custom_call_target="tpu_custom_call" | custom-call | tf_op jit(solution)/shard_map/pallas_call | solution.py:591
  71.5 0.0 copy-start
  71.5 3.2 %copy.8 = bf16[1,256,4096]{2,1,0:T(8,128)(2,1)} copy(bf16[1,256,4096]{2,1,0:T(8,128)(2,1)} %get-tuple-element.4) | data formatting | bytes 4194304
  74.7 0.0 copy-done
  74.7 0.7 copy.9
Async XLA Ops:
  71.5 3.2 %copy-start = (f32[128,512]{1,0:T(8,128)S(1)}, f32[128,512]{1,0:T(8,128)}, u32[]{:S(2)}) copy-start(f32[128,512]{1,0:T(8,128)} %get-tuple-element.5) | copy-start | bytes 786436

commit v5 on v4

--- a/solution.py
+++ b/solution.py
@@ -147,14 +147,13 @@
 ORDER = (
     ("z", 1, 0), ("swap",), ("z", 1, 1), ("a", 1, 0), ("b", 1, 0, 0), ("z", 1, 2), ("a", 1, 1),
     ("b", 1, 1, 0), ("b", 1, 0, 1), ("z", 1, 3), ("prep",), ("b", 1, 2, 0), ("a", 1, 2),
-    ("b", 1, 1, 1), ("b", 1, 3, 0), ("a", 1, 3), ("z", 0, 0), ("take",), ("d", 1, 0),
-    ("b", 1, 2, 1), ("d", 1, 1), ("z", 0, 1), ("b", 1, 3, 1), ("d", 1, 2), ("z", 0, 2),
-    ("d", 1, 3), ("partial", 1), ("a", 0, 0), ("b", 0, 0, 0), ("halo",), ("z", 0, 3),
-    ("b", 0, 1, 0), ("b", 0, 2, 0), ("a", 0, 1), ("a", 0, 2), ("b", 0, 0, 1), ("d", 0, 0),
-    ("b", 0, 2, 1), ("a", 0, 3), ("b", 0, 3, 0), ("b", 0, 1, 1), ("d", 0, 1), ("d", 0, 2),
-    ("values",), ("b", 0, 3, 1), ("d", 0, 3), ("partial", 0),
+    ("b", 1, 1, 1), ("b", 1, 3, 0), ("a", 1, 3), ("z", 0, 0), ("take",),
+    ("b", 1, 2, 1), ("z", 0, 1), ("b", 1, 3, 1), ("d", 1, 0, 4), ("partial", 1), ("z", 0, 2),
+    ("a", 0, 0), ("b", 0, 0, 0), ("halo",), ("z", 0, 3),
+    ("b", 0, 1, 0), ("b", 0, 2, 0), ("a", 0, 1), ("a", 0, 2), ("b", 0, 0, 1),
+    ("b", 0, 2, 1), ("a", 0, 3), ("b", 0, 3, 0), ("values",), ("b", 0, 1, 1),
+    ("d", 0, 0, 3), ("b", 0, 3, 1), ("d", 0, 3, 4), ("partial", 0),
 )
-CHUNKS = (2, 1, 3, 0)
 
 
 def dot_nn(a, b):
@@ -186,8 +185,8 @@
 
 def fused(
     x_hbm, doc_hbm, w_hbm, do_hbm, dx_hbm, g_ref,
-    xo, xs, docv, wv, acc, pacc, qs, qt, dos, dot_, pgs, kv, dkv, pst, dst_, gp, gpt, dxo, dxr,
-    gb, rb, sa, ra, sz, rz, kz,
+    xo, xs, docv, vis, wv, acc, pacc, qs, qt, dos, dot_, pgs, kv, dkv, pst, dst_, gp, gpt, dxo, dxr,
+    gb, rb, sa, ra, sz, rz,
     lsem, xsem, wsend, wrecv, hsend, hrecv, ssend, srecv, gsend, grecv, osem,
 ):
     s = lax.axis_index("seq")
@@ -337,13 +336,19 @@
     def stage_b(h, k, a):
         arrived(h, block_at(h, k, 1, a), 8 + 2 * k + a)
 
-    def stage_d(h, k):
-        zz = z_order[k]
-        part = dot_nn(xo[zz], wv[h, zz].reshape(span, half))
-        if k == 0:
-            acc[h] = part
-        else:
-            acc[h] += part
+    def stage_d(h, low, high):
+        def one(j, carry):
+            zz = jnp.where(
+                j == 0,
+                z_order[0],
+                jnp.where(j == 1, z_order[1], jnp.where(j == 2, z_order[2], z_order[3])),
+            )
+            acc[h] += dot_nn(xo[zz], wv[h, zz].reshape(span, half))
+            return carry
+
+        if low == 0:
+            acc[h] = jnp.zeros_like(acc[h])
+        lax.fori_loop(low, high, one, 0)
 
     def projected(h):
         swaps[4 + h].wait_recv()
@@ -367,8 +372,10 @@
         def _():
             halo.wait_recv()
 
-        for j in range(2):
+        def one(j):
             pgs[j] = dot_nt(dos[...], kv[j, :, hd:])
+
+        each(2, one)
 
     for stage, *at in ORDER:
         if stage == "z":
@@ -399,20 +406,21 @@
             doc = jnp.broadcast_to(docv[...], (tok, tok)).T
             row = lax.broadcasted_iota(jnp.int32, (tok, tok), 0)
             col = lax.broadcasted_iota(jnp.int32, (tok, tok), 1)
-            vis_own = jnp.where((col <= row) & (col + s * tok >= doc), 0.0, -jnp.inf)
-            vis_pri = jnp.where((col > row) & (col + (s - 1) * tok >= doc), 0.0, -jnp.inf)
+            vis[1] = jnp.where((col <= row) & (col + s * tok >= doc), 0.0, -jnp.inf)
+            vis[0] = jnp.where((col > row) & (col + (s - 1) * tok >= doc), 0.0, -jnp.inf)
             dot_[...] = dos[...].T
 
     q_own = projected(0)
     for h in range(2):
         qs[h * tok : (h + 1) * tok, :] = q_own[:, h * hd : (h + 1) * hd]
     qt[...] = qs[...].T
-    k_own = kv[1, :, :hd]
-    k_pri = kv[0, :, :hd]
-    for h in range(2):
-        at = slice(h * tok, (h + 1) * tok)
-        s_own = dot_nt(qs[at, :], k_own) * inv_root + vis_own
-        s_pri = dot_nt(qs[at, :], k_pri) * inv_root + vis_pri
+
+    def attend(h):
+        k_own = kv[1, :, :hd]
+        k_pri = kv[0, :, :hd]
+        at = pl.ds(pl.multiple_of(h * tok, tok), tok)
+        s_own = dot_nt(qs[at, :], k_own) * inv_root + vis[1]
+        s_pri = dot_nt(qs[at, :], k_pri) * inv_root + vis[0]
         pg_own = pgs[1, at, :]
         pg_pri = pgs[0, at, :]
         top = jnp.max(jnp.maximum(s_own, s_pri), axis=1, keepdims=True)
@@ -431,6 +439,8 @@
         dst_[0, at, :] = (p_pri * (pg_pri - row_dot)).astype(BF)
         dst_[1, at, :] = (p_own * (pg_own - row_dot)).astype(BF)
 
+    each(2, attend)
+
     dkv[0, :hd, :] = (dot_nn(qt[...], dst_[0]) * inv_root).astype(BF)
     dkv[0, hd:, :] = dot_nn(dot_[...], pst[0]).astype(BF)
     back = remote(dkv.at[0], dkv.at[1], hsend.at[1], hrecv.at[1], ((s + 7) % 8, d))
@@ -443,13 +453,11 @@
     def _():
         dkv[1] = jnp.zeros_like(dkv[1])
 
+    dq = (
+        (dot_nn(dst_[1], kv[1, :, :hd]) + dot_nn(dst_[0], kv[0, :, :hd])) * inv_root
+    ).astype(BF)
     for h in range(2):
-        at = slice(h * tok, (h + 1) * tok)
-        gp[0, :tok, h * hd : (h + 1) * hd] = (
-            (dot_nn(dst_[1, at, :], k_own) + dot_nn(dst_[0, at, :], k_pri)) * inv_root
-        ).astype(BF)
-
-    rsent = {}
+        gp[0, :tok, h * hd : (h + 1) * hd] = dq[h * tok : (h + 1) * tok]
 
     def swap_grads(h):
         swap(gp.at[h, pl.ds(0, tok)], gp.at[h, pl.ds(tok, tok)], 6 + h)
@@ -458,40 +466,40 @@
         swaps[6 + h].wait_recv()
         gpt[h, :, tok:] = gp[h, tok:, :].T
 
-    def rpush(src, dst, h, k, stage, dev):
-        index = (h * NZ + k) * 3 + stage
-        copy = remote(src, dst, gsend.at[index], grecv.at[index], dev)
-        copy.start()
-        rsent[h, k, stage] = copy
-
-    def produce(h, k):
-        part = dot_nn(gpt[h], xo[(z + k) % NZ]).astype(BF)
+    def chunk(h, i, stage):
+        src, dst, dev = {
+            0: (gb.at[h, i, 1 - my_b], rb.at[h, i], part_b),
+            1: (sa.at[h, i], ra.at[h, i], part_a),
+            2: (sz.at[h, i], rz.at[h, i], ((z + i + 1) % NZ * 2 + y, d)),
+        }[stage]
+        index = (h * NZ + i) * 3 + stage
+        return remote(src, dst, gsend.at[index], grecv.at[index], dev)
+
+    def produce(h, i):
+        part = dot_nn(gpt[h], xo[(z + i + 1) % NZ]).astype(BF)
         for q in range(4):
-            gb[h, k, q // 2, q % 2] = part[:, q * rows : (q + 1) * rows]
-        rpush(gb.at[h, k, 1 - my_b], rb.at[h, k], h, k, 0, part_b)
-
-    def sum_b(h, k, a_at):
-        return gb[h, k, my_b, a_at].astype(F32) + rb[h, k, a_at].astype(F32)
-
-    def send_a(h, k):
-        rsent[h, k, 0].wait_recv()
-        sa[h, k] = sum_b(h, k, 1 - my_a).astype(BF)
-        rpush(sa.at[h, k], ra.at[h, k], h, k, 1, part_a)
-
-    def send_z(h, k):
-        rsent[h, k, 1].wait_recv()
-        total = sum_b(h, k, my_a) + ra[h, k].astype(F32)
-        if k:
-            sz[h, k] = total.astype(BF)
-            rpush(sz.at[h, k], rz.at[h, k], h, k, 2, zdev[k])
-        else:
-            kz[h] = total
+            gb[h, i, q // 2, q % 2] = part[:, q * rows : (q + 1) * rows]
+        chunk(h, i, 0).start()
+
+    def sum_b(h, i, a_at):
+        return gb[h, i, my_b, a_at].astype(F32) + rb[h, i, a_at].astype(F32)
+
+    def send_a(h, i):
+        chunk(h, i, 0).wait_recv()
+        sa[h, i] = sum_b(h, i, 1 - my_a).astype(BF)
+        chunk(h, i, 1).start()
+
+    def send_z(h, i):
+        chunk(h, i, 1).wait_recv()
+        sz[h, i] = (sum_b(h, i, my_a) + ra[h, i].astype(F32)).astype(BF)
+        chunk(h, i, 2).start()
 
     def finish(h):
-        total = kz[h]
-        for k in CHUNKS[:3]:
-            rsent[h, k, 2].wait_recv()
-            total += rz[h, k].astype(F32)
+        chunk(h, NZ - 1, 1).wait_recv()
+        total = sum_b(h, NZ - 1, my_a) + ra[h, NZ - 1].astype(F32)
+        for i in range(NZ - 1):
+            chunk(h, i, 2).wait_recv()
+            total += rz[h, i].astype(F32)
         g_ref[:, h * half : (h + 1) * half] = total.T
 
     def store(src, plane, zz, q, index):
@@ -501,31 +509,30 @@
             osem.at[index],
         )
 
-    stores = []
+    def swap_dx(zz):
+        return remote(
+            dxo.at[zz, pl.ds(tok, tok)], dxr.at[zz], ssend.at[8 + zz], srecv.at[8 + zz], sib
+        )
 
     def input_grad(zz):
         part = dot_nt(gp[0], wv[0, zz].reshape(span, half))
         part += dot_nt(gp[1], wv[1, zz].reshape(span, half))
         dxo[zz] = part.astype(BF)
-        swap(dxo.at[zz, pl.ds(tok, tok)], dxr.at[zz], 8 + zz)
+        swap_dx(zz).start()
         for q in range(4):
-            stores.append(store(dxo, c, zz, q, zz * 4 + q))
-            stores[-1].start()
+            store(dxo, c, zz, q, zz * 4 + q).start()
 
     def take_input_grad(zz):
-        swaps[8 + zz].wait_recv()
+        swap_dx(zz).wait_recv()
         for q in range(4):
-            stores.append(store(dxr, 1 - c, zz, q, 16 + zz * 4 + q))
-            stores[-1].start()
-
-    c0, c1, c2, c3 = CHUNKS
+            store(dxr, 1 - c, zz, q, 16 + zz * 4 + q).start()
+
     swap_grads(0)
     gpt[0, :, :tok] = gp[0, :tok, :].T
     own_dk = dot_nn(qt[...], dst_[1]) * inv_root
     own_dv = dot_nn(dot_[...], pst[1])
     take_grads(0)
-    for k in CHUNKS:
-        produce(0, k)
+    each(NZ, lambda i: produce(0, i))
 
     @pl.when(s < 7)
     def _():
@@ -535,39 +542,50 @@
     gpt[1, hd:, :tok] = (own_dv + dkv[1, hd:, :].astype(F32)).astype(BF)
     gp[1, :tok, :] = gpt[1, :, :tok].T
     swap_grads(1)
-    send_a(0, c0)
     take_grads(1)
-    produce(1, c0)
-    send_a(0, c1)
-    produce(1, c1)
-    send_z(0, c0)
-    send_a(0, c2)
-    produce(1, c2)
-    send_z(0, c1)
-    send_a(0, c3)
-    produce(1, c3)
-    input_grad(0)
-    send_z(0, c2)
-    input_grad(1)
-    send_a(1, c0)
-    send_z(0, c3)
-    input_grad(2)
-    send_a(1, c1)
-    send_z(1, c0)
-    input_grad(3)
-    for zz in range(NZ):
-        take_input_grad(zz)
-    send_a(1, c2)
-    send_z(1, c1)
+
+    def both(i):
+        produce(1, i)
+        send_a(0, i)
+
+    each(NZ, both)
+
+    def spread(i):
+        input_grad(i)
+
+        @pl.when(i < NZ - 1)
+        def _():
+            send_z(0, i)
+
+    each(NZ, spread)
+
+    def tail(i):
+        take_input_grad(i)
+        send_a(1, i)
+
+        @pl.when(i > 0)
+        def _():
+            send_z(1, i - 1)
+
+    each(NZ, tail)
     finish(0)
-    send_a(1, c3)
-    send_z(1, c2)
-    send_z(1, c3)
     finish(1)
 
-    for copy in stores:
-        copy.wait()
-    for copy in sent + list(rsent.values()):
+    def drain(i):
+        swap_dx(i).wait_send()
+        for q in range(4):
+            store(dxo, c, i, q, i * 4 + q).wait()
+            store(dxr, 1 - c, i, q, 16 + i * 4 + q).wait()
+        for h in range(2):
+            chunk(h, i, 0).wait_send()
+            chunk(h, i, 1).wait_send()
+
+            @pl.when(i < NZ - 1)
+            def _():
+                chunk(h, i, 2).wait_send()
+
+    each(NZ, drain)
+    for copy in sent:
         copy.wait_send()
     for copy, test in line:
         pl.when(test)(copy.wait_send)
@@ -603,6 +621,7 @@
             pltpu.VMEM((NZ, 2 * tok, 4 * rows), BF),
             pltpu.VMEM((NZ, tok, 4 * rows), BF),
             pltpu.VMEM((1, tok), jnp.int32),
+            pltpu.VMEM((2, tok, tok), F32),
             pltpu.VMEM((2, NZ, 2, 2, rows, half), BF),
             pltpu.VMEM((2, 2 * tok, half), F32),
             pltpu.VMEM((2, tok, half), F32),
@@ -625,7 +644,6 @@
             pltpu.VMEM((2, NZ) + block, BF),
             pltpu.VMEM((2, NZ) + block, BF),
             pltpu.VMEM((2, NZ) + block, BF),
-            pltpu.VMEM((2,) + block, F32),
             dma((5,)),
             dma((32,)),
             dma((2, 20)),

time: 75.6 us -> 74.6 us (0.987)
  Pallas kernels: 70.9 us -> 69.9 us
    pallas_call x1, Pallas kernels: 70.9 us -> 69.9 us  [kernel_body(): pl.pallas_call(fused, out_shape=(jax.ShapeDtypeStruct(layer_inputs.shape,...]
where the time goes in v5:
time: 74.6 us; the launch traced here: 74.4 us
  Pallas kernels  69.9 us (94%)
  local copies, waits for them, and re-layouts  3.88 us (5%)
    pallas_call x1, Pallas kernels, kernel_body(): pl.pallas_call(fused, out_shape=(jax.ShapeDtypeStruct(layer_inputs.shape,...  69.9 us
    unnamed x4, local copies, waits for them, and re-layouts  3.88 us

profile of v5, /device:TPU:0, one launch (start us, length us, event | category | flops | bytes accessed | tf_op | source)
XLA Modules:
  0.0 74.4 jit_solution(4523815994509096335)
XLA Ops:
  0.6 69.9 %shard_map.59 = (bf16[1,256,4096]{2,1,0:T(8,128)(2,1)}, f32[128,512]{1,0:T(8,128)}) custom-call(bf16[1,256,4096]{2,1,0:T(8,128)(2,1)} %x_hbm.1, s32[1,256]{1,0:T(1,128)} %doc_hbm.1, bf16[128,512]{1,0:T(8,128)(2,1)} %w_hbm.1, bf16[1,256,256]{2,1,0:T(8,128)(2,1)} %do_hbm.1), custom_call_target="tpu_custom_call" | custom-call | tf_op jit(solution)/shard_map/pallas_call | solution.py:609
  70.5 0.0 copy-start
  70.5 3.2 %copy.8 = bf16[1,256,4096]{2,1,0:T(8,128)(2,1)} copy(bf16[1,256,4096]{2,1,0:T(8,128)(2,1)} %get-tuple-element.4) | data formatting | bytes 4194304
  73.7 0.0 copy-done
  73.7 0.7 copy.9
Async XLA Ops:
  70.5 3.2 %copy-start = (f32[128,512]{1,0:T(8,128)S(1)}, f32[128,512]{1,0:T(8,128)}, u32[]{:S(2)}) copy-start(f32[128,512]{1,0:T(8,128)} %get-tuple-element.5) | copy-start | bytes 786436

commit v6 on v5

--- a/solution.py
+++ b/solution.py
@@ -415,12 +415,15 @@
         qs[h * tok : (h + 1) * tok, :] = q_own[:, h * hd : (h + 1) * hd]
     qt[...] = qs[...].T
 
-    def attend(h):
+    part_rows = tok // 2
+
+    def attend(j):
         k_own = kv[1, :, :hd]
         k_pri = kv[0, :, :hd]
-        at = pl.ds(pl.multiple_of(h * tok, tok), tok)
-        s_own = dot_nt(qs[at, :], k_own) * inv_root + vis[1]
-        s_pri = dot_nt(qs[at, :], k_pri) * inv_root + vis[0]
+        at = pl.ds(pl.multiple_of(j * part_rows, part_rows), part_rows)
+        seen = pl.ds(pl.multiple_of(j % 2 * part_rows, part_rows), part_rows)
+        s_own = dot_nt(qs[at, :], k_own) * inv_root + vis[1, seen, :]
+        s_pri = dot_nt(qs[at, :], k_pri) * inv_root + vis[0, seen, :]
         pg_own = pgs[1, at, :]
         pg_pri = pgs[0, at, :]
         top = jnp.max(jnp.maximum(s_own, s_pri), axis=1, keepdims=True)
@@ -439,7 +442,7 @@
         dst_[0, at, :] = (p_pri * (pg_pri - row_dot)).astype(BF)
         dst_[1, at, :] = (p_own * (pg_own - row_dot)).astype(BF)
 
-    each(2, attend)
+    each(4, attend)
 
     dkv[0, :hd, :] = (dot_nn(qt[...], dst_[0]) * inv_root).astype(BF)
     dkv[0, hd:, :] = dot_nn(dot_[...], pst[0]).astype(BF)
@@ -551,23 +554,19 @@
     each(NZ, both)
 
     def spread(i):
-        input_grad(i)
-
         @pl.when(i < NZ - 1)
         def _():
             send_z(0, i)
 
-    each(NZ, spread)
-
-    def tail(i):
-        take_input_grad(i)
+        input_grad(i)
         send_a(1, i)
 
         @pl.when(i > 0)
         def _():
             send_z(1, i - 1)
 
-    each(NZ, tail)
+    each(NZ, spread)
+    each(NZ, take_input_grad)
     finish(0)
     finish(1)
 

time: 74.6 us -> 76.1 us (1.020)
  Pallas kernels: 69.9 us -> 71.4 us
    pallas_call x1, Pallas kernels: 69.9 us -> 71.4 us  [kernel_body(): pl.pallas_call(fused, out_shape=(jax.ShapeDtypeStruct(layer_inputs.shape,...]
where the time goes in v6:
time: 76.1 us; the launch traced here: 75.9 us
  Pallas kernels  71.4 us (94%)
  local copies, waits for them, and re-layouts  3.88 us (5%)
    pallas_call x1, Pallas kernels, kernel_body(): pl.pallas_call(fused, out_shape=(jax.ShapeDtypeStruct(layer_inputs.shape,...  71.4 us
    unnamed x4, local copies, waits for them, and re-layouts  3.88 us

profile of v6, /device:TPU:0, one launch (start us, length us, event | category | flops | bytes accessed | tf_op | source)
XLA Modules:
  0.0 75.9 jit_solution(15302508542429005467)
XLA Ops:
  0.6 71.4 %shard_map.59 = (bf16[1,256,4096]{2,1,0:T(8,128)(2,1)}, f32[128,512]{1,0:T(8,128)}) custom-call(bf16[1,256,4096]{2,1,0:T(8,128)(2,1)} %x_hbm.1, s32[1,256]{1,0:T(1,128)} %doc_hbm.1, bf16[128,512]{1,0:T(8,128)(2,1)} %w_hbm.1, bf16[1,256,256]{2,1,0:T(8,128)(2,1)} %do_hbm.1), custom_call_target="tpu_custom_call" | custom-call | tf_op jit(solution)/shard_map/pallas_call | solution.py:608
  72.1 0.0 copy-start
  72.1 3.2 %copy.8 = bf16[1,256,4096]{2,1,0:T(8,128)(2,1)} copy(bf16[1,256,4096]{2,1,0:T(8,128)(2,1)} %get-tuple-element.4) | data formatting | bytes 4194304
  75.2 0.0 copy-done
  75.2 0.7 copy.9
Async XLA Ops:
  72.1 3.2 %copy-start = (f32[128,512]{1,0:T(8,128)S(1)}, f32[128,512]{1,0:T(8,128)}, u32[]{:S(2)}) copy-start(f32[128,512]{1,0:T(8,128)} %get-tuple-element.5) | copy-start | bytes 786436

commit v7 on v6

--- a/solution.py
+++ b/solution.py
@@ -145,14 +145,10 @@
 F32 = jnp.float32
 NZ = 4
 ORDER = (
-    ("z", 1, 0), ("swap",), ("z", 1, 1), ("a", 1, 0), ("b", 1, 0, 0), ("z", 1, 2), ("a", 1, 1),
-    ("b", 1, 1, 0), ("b", 1, 0, 1), ("z", 1, 3), ("prep",), ("b", 1, 2, 0), ("a", 1, 2),
-    ("b", 1, 1, 1), ("b", 1, 3, 0), ("a", 1, 3), ("z", 0, 0), ("take",),
-    ("b", 1, 2, 1), ("z", 0, 1), ("b", 1, 3, 1), ("d", 1, 0, 4), ("partial", 1), ("z", 0, 2),
-    ("a", 0, 0), ("b", 0, 0, 0), ("halo",), ("z", 0, 3),
-    ("b", 0, 1, 0), ("b", 0, 2, 0), ("a", 0, 1), ("a", 0, 2), ("b", 0, 0, 1),
-    ("b", 0, 2, 1), ("a", 0, 3), ("b", 0, 3, 0), ("values",), ("b", 0, 1, 1),
-    ("d", 0, 0, 3), ("b", 0, 3, 1), ("d", 0, 3, 4), ("partial", 0),
+    ("z", 0), ("swap",), ("z", 1), ("a", 0), ("b", 0, 0), ("z", 2), ("a", 1), ("b", 1, 0),
+    ("b", 0, 1), ("z", 3), ("prep",), ("a", 2), ("b", 2, 0), ("b", 1, 1), ("a", 3), ("take",),
+    ("d", 0, 2), ("b", 3, 0), ("b", 2, 1), ("d", 2, 3), ("b", 3, 1), ("d", 3, 4),
+    ("partial", 1), ("partial", 0), ("halo",), ("values",),
 )
 
 
@@ -194,7 +190,7 @@
     z, y = s // 2, s % 2
     x, c = d // 2, d % 2
     tok = xs.shape[1]
-    rows = wv.shape[4]
+    rows = wv.shape[3]
     hd = qs.shape[1]
     half = 2 * hd
     span = 4 * rows
@@ -246,20 +242,14 @@
 
         lax.fori_loop(0, count, one, 0)
 
-    loads = [
-        pltpu.make_async_copy(
-            w_hbm.at[:, pl.ds(h * half, half)], wv.at[h, z, my_b, my_a], lsem.at[h]
-        )
-        for h in (1, 0)
-    ]
+    load_w = pltpu.make_async_copy(w_hbm, wv.at[z, my_b, my_a], lsem.at[0])
     late = [pltpu.make_async_copy(doc_hbm, docv, lsem.at[2])] + [
         pltpu.make_async_copy(
             do_hbm.at[0, :, pl.ds(h * hd, hd)], dos.at[pl.ds(h * tok, tok)], lsem.at[3 + h]
         )
         for h in range(2)
     ]
-    for load in loads:
-        load.start()
+    load_w.start()
     each(16, lambda j: load_swap(j).start())
     each(16, lambda j: load_own(j).start())
     for load in late:
@@ -283,8 +273,7 @@
             barrier, inc=1, device_id=(s - 1, d), device_id_type=pl.DeviceIdType.MESH
         )
 
-    loads[0].wait()
-    loads[1].wait()
+    load_w.wait()
 
     @pl.when(extra_up | extra_down)
     def _():
@@ -304,50 +293,52 @@
         sent.append(copy)
         swaps[index] = copy
 
-    def block_at(h, k, b_flip, a_flip):
-        return wv.at[h, z_order[k], flip(my_b, b_flip), flip(my_a, a_flip)]
-
-    def push(h, ref, dev, index):
-        copy = remote(ref, ref, wsend.at[h, index], wrecv.at[h, index], dev)
+    def block_at(k, b_flip, a_flip):
+        return wv.at[z_order[k], flip(my_b, b_flip), flip(my_a, a_flip)]
+
+    def push(ref, dev, index):
+        copy = remote(ref, ref, wsend.at[index], wrecv.at[index], dev)
         copy.start()
         sent.append(copy)
 
-    def arrived(h, ref, index):
-        remote(ref, ref, wsend.at[h, 0], wrecv.at[h, index], sib).wait_recv()
-
-    def stage_z(h, k):
-        ref = block_at(h, k, 0, 0)
+    def arrived(ref, index):
+        remote(ref, ref, wsend.at[0], wrecv.at[index], sib).wait_recv()
+
+    def stage_z(k):
+        ref = block_at(k, 0, 0)
         zz = z_order[k]
         if k:
-            arrived(h, ref, zz)
-        up = remote(ref, ref, wsend.at[h, zz], wrecv.at[h, zz], zdev[1])
-        down = remote(ref, ref, wsend.at[h, 16 + zz], wrecv.at[h, zz], zdev[3])
+            arrived(ref, zz)
+        up = remote(ref, ref, wsend.at[zz], wrecv.at[zz], zdev[1])
+        down = remote(ref, ref, wsend.at[16 + zz], wrecv.at[zz], zdev[3])
         for copy, test in ((up, (zz <= z) & (z < NZ - 1)), (down, (zz >= z) & (z > 0))):
             line.append((copy, test))
             pl.when(test)(copy.start)
-        push(h, ref, part_a, 4 + k)
-        push(h, ref, part_b, 8 + 2 * k)
-
-    def stage_a(h, k):
-        ref = block_at(h, k, 0, 1)
-        arrived(h, ref, 4 + k)
-        push(h, ref, part_b, 9 + 2 * k)
-
-    def stage_b(h, k, a):
-        arrived(h, block_at(h, k, 1, a), 8 + 2 * k + a)
-
-    def stage_d(h, low, high):
+        push(ref, part_a, 4 + k)
+        push(ref, part_b, 8 + 2 * k)
+
+    def stage_a(k):
+        ref = block_at(k, 0, 1)
+        arrived(ref, 4 + k)
+        push(ref, part_b, 9 + 2 * k)
+
+    def stage_b(k, a):
+        arrived(block_at(k, 1, a), 8 + 2 * k + a)
+
+    def stage_d(low, high):
         def one(j, carry):
             zz = jnp.where(
                 j == 0,
                 z_order[0],
                 jnp.where(j == 1, z_order[1], jnp.where(j == 2, z_order[2], z_order[3])),
             )
-            acc[h] += dot_nn(xo[zz], wv[h, zz].reshape(span, half))
+            for h in (1, 0):
+                ws = wv[zz, :, :, :, h * half : (h + 1) * half].reshape(span, half)
+                acc[h] += dot_nn(xo[zz], ws)
             return carry
 
         if low == 0:
-            acc[h] = jnp.zeros_like(acc[h])
+            acc[...] = jnp.zeros_like(acc)
         lax.fori_loop(low, high, one, 0)
 
     def projected(h):
@@ -368,14 +359,17 @@
             kv[0] = jnp.zeros_like(kv[0])
 
     def value_grads():
+        pgs[1] = dot_nt(dos[...], kv[1, :, hd:])
+        q_own = projected(0)
+        for h in range(2):
+            qs[h * tok : (h + 1) * tok, :] = q_own[:, h * hd : (h + 1) * hd]
+        qt[...] = qs[...].T
+
         @pl.when(s > 0)
         def _():
             halo.wait_recv()
 
-        def one(j):
-            pgs[j] = dot_nt(dos[...], kv[j, :, hd:])
-
-        each(2, one)
+        pgs[0] = dot_nt(dos[...], kv[0, :, hd:])
 
     for stage, *at in ORDER:
         if stage == "z":
@@ -410,11 +404,6 @@
             vis[0] = jnp.where((col > row) & (col + (s - 1) * tok >= doc), 0.0, -jnp.inf)
             dot_[...] = dos[...].T
 
-    q_own = projected(0)
-    for h in range(2):
-        qs[h * tok : (h + 1) * tok, :] = q_own[:, h * hd : (h + 1) * hd]
-    qt[...] = qs[...].T
-
     part_rows = tok // 2
 
     def attend(j):
@@ -469,39 +458,46 @@
         swaps[6 + h].wait_recv()
         gpt[h, :, tok:] = gp[h, tok:, :].T
 
-    def chunk(h, i, stage):
-        src, dst, dev = {
-            0: (gb.at[h, i, 1 - my_b], rb.at[h, i], part_b),
-            1: (sa.at[h, i], ra.at[h, i], part_a),
-            2: (sz.at[h, i], rz.at[h, i], ((z + i + 1) % NZ * 2 + y, d)),
-        }[stage]
-        index = (h * NZ + i) * 3 + stage
-        return remote(src, dst, gsend.at[index], grecv.at[index], dev)
-
-    def produce(h, i):
-        part = dot_nn(gpt[h], xo[(z + i + 1) % NZ]).astype(BF)
-        for q in range(4):
-            gb[h, i, q // 2, q % 2] = part[:, q * rows : (q + 1) * rows]
-        chunk(h, i, 0).start()
-
-    def sum_b(h, i, a_at):
-        return gb[h, i, my_b, a_at].astype(F32) + rb[h, i, a_at].astype(F32)
-
-    def send_a(h, i):
-        chunk(h, i, 0).wait_recv()
-        sa[h, i] = sum_b(h, i, 1 - my_a).astype(BF)
-        chunk(h, i, 1).start()
-
-    def send_z(h, i):
-        chunk(h, i, 1).wait_recv()
-        sz[h, i] = (sum_b(h, i, my_a) + ra[h, i].astype(F32)).astype(BF)
-        chunk(h, i, 2).start()
+    def to_b(h, p):
+        at = h * 2 + p
+        return remote(gb.at[h, p, 1 - my_b], rb.at[h, p], gsend.at[at], grecv.at[at], part_b)
+
+    def to_a(h, p):
+        at = 4 + h * 2 + p
+        return remote(sa.at[h, p], ra.at[h, p], gsend.at[at], grecv.at[at], part_a)
+
+    def to_z(h, i):
+        at = 8 + h * 3 + i
+        dev = ((z + i + 1) % NZ * 2 + y, d)
+        return remote(sz.at[h, i], rz.at[h, i], gsend.at[at], grecv.at[at], dev)
+
+    def produce(h, p):
+        for e in range(2):
+            part = dot_nn(gpt[h], xo[(z + p * 2 + e + 1) % NZ]).astype(BF)
+            for q in range(4):
+                gb[h, p, q // 2, q % 2, e] = part[:, q * rows : (q + 1) * rows]
+        to_b(h, p).start()
+
+    def sum_b(h, p, a_at, e):
+        return gb[h, p, my_b, a_at, e].astype(F32) + rb[h, p, a_at, e].astype(F32)
+
+    def send_a(h, p):
+        to_b(h, p).wait_recv()
+        for e in range(2):
+            sa[h, p, e] = sum_b(h, p, 1 - my_a, e).astype(BF)
+        to_a(h, p).start()
+
+    def send_z(h, p):
+        to_a(h, p).wait_recv()
+        for e in range(2 - p):
+            i = p * 2 + e
+            sz[h, i] = (sum_b(h, p, my_a, e) + ra[h, p, e].astype(F32)).astype(BF)
+            to_z(h, i).start()
 
     def finish(h):
-        chunk(h, NZ - 1, 1).wait_recv()
-        total = sum_b(h, NZ - 1, my_a) + ra[h, NZ - 1].astype(F32)
+        total = sum_b(h, 1, my_a, 1) + ra[h, 1, 1].astype(F32)
         for i in range(NZ - 1):
-            chunk(h, i, 2).wait_recv()
+            to_z(h, i).wait_recv()
             total += rz[h, i].astype(F32)
         g_ref[:, h * half : (h + 1) * half] = total.T
 
@@ -518,8 +514,8 @@
         )
 
     def input_grad(zz):
-        part = dot_nt(gp[0], wv[0, zz].reshape(span, half))
-        part += dot_nt(gp[1], wv[1, zz].reshape(span, half))
+        ws = wv[zz].reshape(span, 2 * half)
+        part = dot_nt(gp[0], ws[:, :half]) + dot_nt(gp[1], ws[:, half:])
         dxo[zz] = part.astype(BF)
         swap_dx(zz).start()
         for q in range(4):
@@ -535,7 +531,8 @@
     own_dk = dot_nn(qt[...], dst_[1]) * inv_root
     own_dv = dot_nn(dot_[...], pst[1])
     take_grads(0)
-    each(NZ, lambda i: produce(0, i))
+    produce(0, 0)
+    produce(0, 1)
 
     @pl.when(s < 7)
     def _():
@@ -547,26 +544,18 @@
     swap_grads(1)
     take_grads(1)
 
-    def both(i):
-        produce(1, i)
-        send_a(0, i)
-
-    each(NZ, both)
-
-    def spread(i):
-        @pl.when(i < NZ - 1)
-        def _():
-            send_z(0, i)
-
-        input_grad(i)
-        send_a(1, i)
-
-        @pl.when(i > 0)
-        def _():
-            send_z(1, i - 1)
-
-    each(NZ, spread)
+    for p in range(2):
+        produce(1, p)
+        send_a(0, p)
+    send_z(0, 0)
+    lax.fori_loop(0, 2, lambda i, carry: (input_grad(i), carry)[1], 0)
+    send_a(1, 0)
+    send_z(0, 1)
+    lax.fori_loop(2, 4, lambda i, carry: (input_grad(i), carry)[1], 0)
+    send_a(1, 1)
+    send_z(1, 0)
     each(NZ, take_input_grad)
+    send_z(1, 1)
     finish(0)
     finish(1)
 
@@ -575,17 +564,16 @@
         for q in range(4):
             store(dxo, c, i, q, i * 4 + q).wait()
             store(dxr, 1 - c, i, q, 16 + i * 4 + q).wait()
-        for h in range(2):
-            chunk(h, i, 0).wait_send()
-            chunk(h, i, 1).wait_send()
-
-            @pl.when(i < NZ - 1)
-            def _():
-                chunk(h, i, 2).wait_send()
 
     each(NZ, drain)
     for copy in sent:
         copy.wait_send()
+    for h in range(2):
+        for p in range(2):
+            to_b(h, p).wait_send()
+            to_a(h, p).wait_send()
+        for i in range(NZ - 1):
+            to_z(h, i).wait_send()
     for copy, test in line:
         pl.when(test)(copy.wait_send)
 
@@ -621,7 +609,7 @@
             pltpu.VMEM((NZ, tok, 4 * rows), BF),
             pltpu.VMEM((1, tok), jnp.int32),
             pltpu.VMEM((2, tok, tok), F32),
-            pltpu.VMEM((2, NZ, 2, 2, rows, half), BF),
+            pltpu.VMEM((NZ, 2, 2, rows, cols), BF),
             pltpu.VMEM((2, 2 * tok, half), F32),
             pltpu.VMEM((2, tok, half), F32),
             pltpu.VMEM((2 * tok, hd), BF),
@@ -637,22 +625,22 @@
             pltpu.VMEM((2, half, 2 * tok), BF),
             pltpu.VMEM((NZ, 2 * tok, 4 * rows), BF),
             pltpu.VMEM((NZ, tok, 4 * rows), BF),
-            pltpu.VMEM((2, NZ, 2, 2) + block, BF),
-            pltpu.VMEM((2, NZ, 2) + block, BF),
-            pltpu.VMEM((2, NZ) + block, BF),
-            pltpu.VMEM((2, NZ) + block, BF),
+            pltpu.VMEM((2, 2, 2, 2, 2) + block, BF),
+            pltpu.VMEM((2, 2, 2, 2) + block, BF),
+            pltpu.VMEM((2, 2, 2) + block, BF),
+            pltpu.VMEM((2, 2, 2) + block, BF),
             pltpu.VMEM((2, NZ) + block, BF),
             pltpu.VMEM((2, NZ) + block, BF),
             dma((5,)),
             dma((32,)),
-            dma((2, 20)),
-            dma((2, 16)),
+            dma((20,)),
+            dma((16,)),
             dma((2,)),
             dma((2,)),
             dma((12,)),
             dma((12,)),
-            dma((24,)),
-            dma((24,)),
+            dma((14,)),
+            dma((14,)),
             dma((32,)),
         ],
         compiler_params=pltpu.CompilerParams(

time: 76.1 us -> 74 us (0.972)
  Pallas kernels: 71.4 us -> 68.7 us
    pallas_call x1, Pallas kernels: 71.4 us -> 68.7 us  [kernel_body(): pl.pallas_call(fused, out_shape=(jax.ShapeDtypeStruct(layer_inputs.shape,...]
where the time goes in v7:
time: 74 us; the launch traced here: 73.2 us
  Pallas kernels  68.7 us (93%)
  local copies, waits for them, and re-layouts  3.88 us (5%)
    pallas_call x1, Pallas kernels, kernel_body(): pl.pallas_call(fused, out_shape=(jax.ShapeDtypeStruct(layer_inputs.shape,...  68.7 us
    unnamed x4, local copies, waits for them, and re-layouts  3.88 us

profile of v7, /device:TPU:0, one launch (start us, length us, event | category | flops | bytes accessed | tf_op | source)
XLA Modules:
  0.0 73.2 jit_solution(16384643463683258343)
XLA Ops:
  0.6 68.7 %shard_map.59 = (bf16[1,256,4096]{2,1,0:T(8,128)(2,1)}, f32[128,512]{1,0:T(8,128)}) custom-call(bf16[1,256,4096]{2,1,0:T(8,128)(2,1)} %x_hbm.1, s32[1,256]{1,0:T(1,128)} %doc_hbm.1, bf16[128,512]{1,0:T(8,128)(2,1)} %w_hbm.1, bf16[1,256,256]{2,1,0:T(8,128)(2,1)} %do_hbm.1), custom_call_target="tpu_custom_call" | custom-call | tf_op jit(solution)/shard_map/pallas_call | solution.py:596
  69.3 0.0 copy-start
  69.3 3.2 %copy.8 = bf16[1,256,4096]{2,1,0:T(8,128)(2,1)} copy(bf16[1,256,4096]{2,1,0:T(8,128)(2,1)} %get-tuple-element.4) | data formatting | bytes 4194304
  72.5 0.0 copy-done
  72.5 0.7 copy.9
Async XLA Ops:
  69.3 3.2 %copy-start = (f32[128,512]{1,0:T(8,128)S(1)}, f32[128,512]{1,0:T(8,128)}, u32[]{:S(2)}) copy-start(f32[128,512]{1,0:T(8,128)} %get-tuple-element.5) | copy-start | bytes 786436

commit v8 on v7

--- a/solution.py
+++ b/solution.py
@@ -145,10 +145,14 @@
 F32 = jnp.float32
 NZ = 4
 ORDER = (
-    ("z", 0), ("swap",), ("z", 1), ("a", 0), ("b", 0, 0), ("z", 2), ("a", 1), ("b", 1, 0),
-    ("b", 0, 1), ("z", 3), ("prep",), ("a", 2), ("b", 2, 0), ("b", 1, 1), ("a", 3), ("take",),
-    ("d", 0, 2), ("b", 3, 0), ("b", 2, 1), ("d", 2, 3), ("b", 3, 1), ("d", 3, 4),
-    ("partial", 1), ("partial", 0), ("halo",), ("values",),
+    ("z", 1, 0), ("swap",), ("z", 1, 1), ("a", 1, 0), ("b", 1, 0, 0), ("z", 1, 2), ("a", 1, 1),
+    ("b", 1, 1, 0), ("b", 1, 0, 1), ("z", 1, 3), ("prep",), ("b", 1, 2, 0), ("a", 1, 2),
+    ("b", 1, 1, 1), ("b", 1, 3, 0), ("a", 1, 3), ("z", 0, 0), ("take",),
+    ("b", 1, 2, 1), ("z", 0, 1), ("b", 1, 3, 1), ("d", 1, 0, 4), ("partial", 1), ("z", 0, 2),
+    ("a", 0, 0), ("b", 0, 0, 0), ("halo",), ("z", 0, 3),
+    ("b", 0, 1, 0), ("b", 0, 2, 0), ("a", 0, 1), ("a", 0, 2), ("b", 0, 0, 1),
+    ("b", 0, 2, 1), ("a", 0, 3), ("b", 0, 3, 0), ("values",), ("b", 0, 1, 1),
+    ("d", 0, 0, 3), ("b", 0, 3, 1), ("d", 0, 3, 4), ("partial", 0),
 )
 
 
@@ -190,7 +194,7 @@
     z, y = s // 2, s % 2
     x, c = d // 2, d % 2
     tok = xs.shape[1]
-    rows = wv.shape[3]
+    rows = wv.shape[4]
     hd = qs.shape[1]
     half = 2 * hd
     span = 4 * rows
@@ -242,14 +246,20 @@
 
         lax.fori_loop(0, count, one, 0)
 
-    load_w = pltpu.make_async_copy(w_hbm, wv.at[z, my_b, my_a], lsem.at[0])
+    loads = [
+        pltpu.make_async_copy(
+            w_hbm.at[:, pl.ds(h * half, half)], wv.at[h, z, my_b, my_a], lsem.at[h]
+        )
+        for h in (1, 0)
+    ]
     late = [pltpu.make_async_copy(doc_hbm, docv, lsem.at[2])] + [
         pltpu.make_async_copy(
             do_hbm.at[0, :, pl.ds(h * hd, hd)], dos.at[pl.ds(h * tok, tok)], lsem.at[3 + h]
         )
         for h in range(2)
     ]
-    load_w.start()
+    for load in loads:
+        load.start()
     each(16, lambda j: load_swap(j).start())
     each(16, lambda j: load_own(j).start())
     for load in late:
@@ -273,7 +283,8 @@
             barrier, inc=1, device_id=(s - 1, d), device_id_type=pl.DeviceIdType.MESH
         )
 
-    load_w.wait()
+    loads[0].wait()
+    loads[1].wait()
 
     @pl.when(extra_up | extra_down)
     def _():
@@ -293,52 +304,50 @@
         sent.append(copy)
         swaps[index] = copy
 
-    def block_at(k, b_flip, a_flip):
-        return wv.at[z_order[k], flip(my_b, b_flip), flip(my_a, a_flip)]
-
-    def push(ref, dev, index):
-        copy = remote(ref, ref, wsend.at[index], wrecv.at[index], dev)
+    def block_at(h, k, b_flip, a_flip):
+        return wv.at[h, z_order[k], flip(my_b, b_flip), flip(my_a, a_flip)]
+
+    def push(h, ref, dev, index):
+        copy = remote(ref, ref, wsend.at[h, index], wrecv.at[h, index], dev)
         copy.start()
         sent.append(copy)
 
-    def arrived(ref, index):
-        remote(ref, ref, wsend.at[0], wrecv.at[index], sib).wait_recv()
-
-    def stage_z(k):
-        ref = block_at(k, 0, 0)
+    def arrived(h, ref, index):
+        remote(ref, ref, wsend.at[h, 0], wrecv.at[h, index], sib).wait_recv()
+
+    def stage_z(h, k):
+        ref = block_at(h, k, 0, 0)
         zz = z_order[k]
         if k:
-            arrived(ref, zz)
-        up = remote(ref, ref, wsend.at[zz], wrecv.at[zz], zdev[1])
-        down = remote(ref, ref, wsend.at[16 + zz], wrecv.at[zz], zdev[3])
+            arrived(h, ref, zz)
+        up = remote(ref, ref, wsend.at[h, zz], wrecv.at[h, zz], zdev[1])
+        down = remote(ref, ref, wsend.at[h, 16 + zz], wrecv.at[h, zz], zdev[3])
         for copy, test in ((up, (zz <= z) & (z < NZ - 1)), (down, (zz >= z) & (z > 0))):
             line.append((copy, test))
             pl.when(test)(copy.start)
-        push(ref, part_a, 4 + k)
-        push(ref, part_b, 8 + 2 * k)
-
-    def stage_a(k):
-        ref = block_at(k, 0, 1)
-        arrived(ref, 4 + k)
-        push(ref, part_b, 9 + 2 * k)
-
-    def stage_b(k, a):
-        arrived(block_at(k, 1, a), 8 + 2 * k + a)
-
-    def stage_d(low, high):
+        push(h, ref, part_a, 4 + k)
+        push(h, ref, part_b, 8 + 2 * k)
+
+    def stage_a(h, k):
+        ref = block_at(h, k, 0, 1)
+        arrived(h, ref, 4 + k)
+        push(h, ref, part_b, 9 + 2 * k)
+
+    def stage_b(h, k, a):
+        arrived(h, block_at(h, k, 1, a), 8 + 2 * k + a)
+
+    def stage_d(h, low, high):
         def one(j, carry):
             zz = jnp.where(
                 j == 0,
                 z_order[0],
                 jnp.where(j == 1, z_order[1], jnp.where(j == 2, z_order[2], z_order[3])),
             )
-            for h in (1, 0):
-                ws = wv[zz, :, :, :, h * half : (h + 1) * half].reshape(span, half)
-                acc[h] += dot_nn(xo[zz], ws)
+            acc[h] += dot_nn(xo[zz], wv[h, zz].reshape(span, half))
             return carry
 
         if low == 0:
-            acc[...] = jnp.zeros_like(acc)
+            acc[h] = jnp.zeros_like(acc[h])
         lax.fori_loop(low, high, one, 0)
 
     def projected(h):
@@ -359,17 +368,14 @@
             kv[0] = jnp.zeros_like(kv[0])
 
     def value_grads():
-        pgs[1] = dot_nt(dos[...], kv[1, :, hd:])
-        q_own = projected(0)
-        for h in range(2):
-            qs[h * tok : (h + 1) * tok, :] = q_own[:, h * hd : (h + 1) * hd]
-        qt[...] = qs[...].T
-
         @pl.when(s > 0)
         def _():
             halo.wait_recv()
 
-        pgs[0] = dot_nt(dos[...], kv[0, :, hd:])
+        def one(j):
+            pgs[j] = dot_nt(dos[...], kv[j, :, hd:])
+
+        each(2, one)
 
     for stage, *at in ORDER:
         if stage == "z":
@@ -404,6 +410,11 @@
             vis[0] = jnp.where((col > row) & (col + (s - 1) * tok >= doc), 0.0, -jnp.inf)
             dot_[...] = dos[...].T
 
+    q_own = projected(0)
+    for h in range(2):
+        qs[h * tok : (h + 1) * tok, :] = q_own[:, h * hd : (h + 1) * hd]
+    qt[...] = qs[...].T
+
     part_rows = tok // 2
 
     def attend(j):
@@ -514,8 +525,8 @@
         )
 
     def input_grad(zz):
-        ws = wv[zz].reshape(span, 2 * half)
-        part = dot_nt(gp[0], ws[:, :half]) + dot_nt(gp[1], ws[:, half:])
+        part = dot_nt(gp[0], wv[0, zz].reshape(span, half))
+        part += dot_nt(gp[1], wv[1, zz].reshape(span, half))
         dxo[zz] = part.astype(BF)
         swap_dx(zz).start()
         for q in range(4):
@@ -609,7 +620,7 @@
             pltpu.VMEM((NZ, tok, 4 * rows), BF),
             pltpu.VMEM((1, tok), jnp.int32),
             pltpu.VMEM((2, tok, tok), F32),
-            pltpu.VMEM((NZ, 2, 2, rows, cols), BF),
+            pltpu.VMEM((2, NZ, 2, 2, rows, half), BF),
             pltpu.VMEM((2, 2 * tok, half), F32),
             pltpu.VMEM((2, tok, half), F32),
             pltpu.VMEM((2 * tok, hd), BF),
@@ -633,8 +644,8 @@
             pltpu.VMEM((2, NZ) + block, BF),
             dma((5,)),
             dma((32,)),
-            dma((20,)),
-            dma((16,)),
+            dma((2, 20)),
+            dma((2, 16)),
             dma((2,)),
             dma((2,)),
             dma((12,)),

time: 74 us -> 79 us (1.068)
  Pallas kernels: 68.7 us -> 74.3 us
    pallas_call x1, Pallas kernels: 68.7 us -> 74.3 us  [kernel_body(): pl.pallas_call(fused, out_shape=(jax.ShapeDtypeStruct(layer_inputs.shape,...]
where the time goes in v8:
time: 79 us; the launch traced here: 78.8 us
  Pallas kernels  74.3 us (94%)
  local copies, waits for them, and re-layouts  3.88 us (5%)
    pallas_call x1, Pallas kernels, kernel_body(): pl.pallas_call(fused, out_shape=(jax.ShapeDtypeStruct(layer_inputs.shape,...  74.3 us
    unnamed x4, local copies, waits for them, and re-layouts  3.88 us

profile of v8, /device:TPU:0, one launch (start us, length us, event | category | flops | bytes accessed | tf_op | source)
XLA Modules:
  0.0 78.8 jit_solution(10557068705094719595)
XLA Ops:
  0.6 74.3 %shard_map.59 = (bf16[1,256,4096]{2,1,0:T(8,128)(2,1)}, f32[128,512]{1,0:T(8,128)}) custom-call(bf16[1,256,4096]{2,1,0:T(8,128)(2,1)} %x_hbm.1, s32[1,256]{1,0:T(1,128)} %doc_hbm.1, bf16[128,512]{1,0:T(8,128)(2,1)} %w_hbm.1, bf16[1,256,256]{2,1,0:T(8,128)(2,1)} %do_hbm.1), custom_call_target="tpu_custom_call" | custom-call | tf_op jit(solution)/shard_map/pallas_call | solution.py:607
  74.9 0.0 copy-start
  75.0 3.2 %copy.8 = bf16[1,256,4096]{2,1,0:T(8,128)(2,1)} copy(bf16[1,256,4096]{2,1,0:T(8,128)(2,1)} %get-tuple-element.4) | data formatting | bytes 4194304
  78.1 0.0 copy-done
  78.1 0.7 copy.9
Async XLA Ops:
  74.9 3.2 %copy-start = (f32[128,512]{1,0:T(8,128)S(1)}, f32[128,512]{1,0:T(8,128)}, u32[]{:S(2)}) copy-start(f32[128,512]{1,0:T(8,128)} %get-tuple-element.5) | copy-start | bytes 786436

commit v9 on v6

--- a/solution.py
+++ b/solution.py
@@ -145,14 +145,10 @@
 F32 = jnp.float32
 NZ = 4
 ORDER = (
-    ("z", 1, 0), ("swap",), ("z", 1, 1), ("a", 1, 0), ("b", 1, 0, 0), ("z", 1, 2), ("a", 1, 1),
-    ("b", 1, 1, 0), ("b", 1, 0, 1), ("z", 1, 3), ("prep",), ("b", 1, 2, 0), ("a", 1, 2),
-    ("b", 1, 1, 1), ("b", 1, 3, 0), ("a", 1, 3), ("z", 0, 0), ("take",),
-    ("b", 1, 2, 1), ("z", 0, 1), ("b", 1, 3, 1), ("d", 1, 0, 4), ("partial", 1), ("z", 0, 2),
-    ("a", 0, 0), ("b", 0, 0, 0), ("halo",), ("z", 0, 3),
-    ("b", 0, 1, 0), ("b", 0, 2, 0), ("a", 0, 1), ("a", 0, 2), ("b", 0, 0, 1),
-    ("b", 0, 2, 1), ("a", 0, 3), ("b", 0, 3, 0), ("values",), ("b", 0, 1, 1),
-    ("d", 0, 0, 3), ("b", 0, 3, 1), ("d", 0, 3, 4), ("partial", 0),
+    ("z", 0), ("swap",), ("z", 1), ("a", 0), ("b", 0, 0), ("z", 2), ("a", 1), ("b", 1, 0),
+    ("b", 0, 1), ("z", 3), ("prep",), ("a", 2), ("b", 2, 0), ("b", 1, 1), ("a", 3), ("take",),
+    ("d", 0, 2), ("b", 3, 0), ("b", 2, 1), ("d", 2, 3), ("b", 3, 1), ("d", 3, 4),
+    ("partial", 1), ("partial", 0), ("halo",), ("values",),
 )
 
 
@@ -194,7 +190,7 @@
     z, y = s // 2, s % 2
     x, c = d // 2, d % 2
     tok = xs.shape[1]
-    rows = wv.shape[4]
+    rows = wv.shape[3]
     hd = qs.shape[1]
     half = 2 * hd
     span = 4 * rows
@@ -246,20 +242,14 @@
 
         lax.fori_loop(0, count, one, 0)
 
-    loads = [
-        pltpu.make_async_copy(
-            w_hbm.at[:, pl.ds(h * half, half)], wv.at[h, z, my_b, my_a], lsem.at[h]
-        )
-        for h in (1, 0)
-    ]
+    load_w = pltpu.make_async_copy(w_hbm, wv.at[z, my_b, my_a], lsem.at[0])
     late = [pltpu.make_async_copy(doc_hbm, docv, lsem.at[2])] + [
         pltpu.make_async_copy(
             do_hbm.at[0, :, pl.ds(h * hd, hd)], dos.at[pl.ds(h * tok, tok)], lsem.at[3 + h]
         )
         for h in range(2)
     ]
-    for load in loads:
-        load.start()
+    load_w.start()
     each(16, lambda j: load_swap(j).start())
     each(16, lambda j: load_own(j).start())
     for load in late:
@@ -283,8 +273,7 @@
             barrier, inc=1, device_id=(s - 1, d), device_id_type=pl.DeviceIdType.MESH
         )
 
-    loads[0].wait()
-    loads[1].wait()
+    load_w.wait()
 
     @pl.when(extra_up | extra_down)
     def _():
@@ -304,50 +293,52 @@
         sent.append(copy)
         swaps[index] = copy
 
-    def block_at(h, k, b_flip, a_flip):
-        return wv.at[h, z_order[k], flip(my_b, b_flip), flip(my_a, a_flip)]
-
-    def push(h, ref, dev, index):
-        copy = remote(ref, ref, wsend.at[h, index], wrecv.at[h, index], dev)
+    def block_at(k, b_flip, a_flip):
+        return wv.at[z_order[k], flip(my_b, b_flip), flip(my_a, a_flip)]
+
+    def push(ref, dev, index):
+        copy = remote(ref, ref, wsend.at[index], wrecv.at[index], dev)
         copy.start()
         sent.append(copy)
 
-    def arrived(h, ref, index):
-        remote(ref, ref, wsend.at[h, 0], wrecv.at[h, index], sib).wait_recv()
-
-    def stage_z(h, k):
-        ref = block_at(h, k, 0, 0)
+    def arrived(ref, index):
+        remote(ref, ref, wsend.at[0], wrecv.at[index], sib).wait_recv()
+
+    def stage_z(k):
+        ref = block_at(k, 0, 0)
         zz = z_order[k]
         if k:
-            arrived(h, ref, zz)
-        up = remote(ref, ref, wsend.at[h, zz], wrecv.at[h, zz], zdev[1])
-        down = remote(ref, ref, wsend.at[h, 16 + zz], wrecv.at[h, zz], zdev[3])
+            arrived(ref, zz)
+        up = remote(ref, ref, wsend.at[zz], wrecv.at[zz], zdev[1])
+        down = remote(ref, ref, wsend.at[16 + zz], wrecv.at[zz], zdev[3])
         for copy, test in ((up, (zz <= z) & (z < NZ - 1)), (down, (zz >= z) & (z > 0))):
             line.append((copy, test))
             pl.when(test)(copy.start)
-        push(h, ref, part_a, 4 + k)
-        push(h, ref, part_b, 8 + 2 * k)
-
-    def stage_a(h, k):
-        ref = block_at(h, k, 0, 1)
-        arrived(h, ref, 4 + k)
-        push(h, ref, part_b, 9 + 2 * k)
-
-    def stage_b(h, k, a):
-        arrived(h, block_at(h, k, 1, a), 8 + 2 * k + a)
-
-    def stage_d(h, low, high):
+        push(ref, part_a, 4 + k)
+        push(ref, part_b, 8 + 2 * k)
+
+    def stage_a(k):
+        ref = block_at(k, 0, 1)
+        arrived(ref, 4 + k)
+        push(ref, part_b, 9 + 2 * k)
+
+    def stage_b(k, a):
+        arrived(block_at(k, 1, a), 8 + 2 * k + a)
+
+    def stage_d(low, high):
         def one(j, carry):
             zz = jnp.where(
                 j == 0,
                 z_order[0],
                 jnp.where(j == 1, z_order[1], jnp.where(j == 2, z_order[2], z_order[3])),
             )
-            acc[h] += dot_nn(xo[zz], wv[h, zz].reshape(span, half))
+            for h in (1, 0):
+                ws = wv[zz, :, :, :, h * half : (h + 1) * half].reshape(span, half)
+                acc[h] += dot_nn(xo[zz], ws)
             return carry
 
         if low == 0:
-            acc[h] = jnp.zeros_like(acc[h])
+            acc[...] = jnp.zeros_like(acc)
         lax.fori_loop(low, high, one, 0)
 
     def projected(h):
@@ -368,14 +359,17 @@
             kv[0] = jnp.zeros_like(kv[0])
 
     def value_grads():
+        pgs[1] = dot_nt(dos[...], kv[1, :, hd:])
+        q_own = projected(0)
+        for h in range(2):
+            qs[h * tok : (h + 1) * tok, :] = q_own[:, h * hd : (h + 1) * hd]
+        qt[...] = qs[...].T
+
         @pl.when(s > 0)
         def _():
             halo.wait_recv()
 
-        def one(j):
-            pgs[j] = dot_nt(dos[...], kv[j, :, hd:])
-
-        each(2, one)
+        pgs[0] = dot_nt(dos[...], kv[0, :, hd:])
 
     for stage, *at in ORDER:
         if stage == "z":
@@ -410,11 +404,6 @@
             vis[0] = jnp.where((col > row) & (col + (s - 1) * tok >= doc), 0.0, -jnp.inf)
             dot_[...] = dos[...].T
 
-    q_own = projected(0)
-    for h in range(2):
-        qs[h * tok : (h + 1) * tok, :] = q_own[:, h * hd : (h + 1) * hd]
-    qt[...] = qs[...].T
-
     part_rows = tok // 2
 
     def attend(j):
@@ -518,8 +507,8 @@
         )
 
     def input_grad(zz):
-        part = dot_nt(gp[0], wv[0, zz].reshape(span, half))
-        part += dot_nt(gp[1], wv[1, zz].reshape(span, half))
+        ws = wv[zz].reshape(span, 2 * half)
+        part = dot_nt(gp[0], ws[:, :half]) + dot_nt(gp[1], ws[:, half:])
         dxo[zz] = part.astype(BF)
         swap_dx(zz).start()
         for q in range(4):
@@ -554,19 +543,23 @@
     each(NZ, both)
 
     def spread(i):
+        input_grad(i)
+
         @pl.when(i < NZ - 1)
         def _():
             send_z(0, i)
 
-        input_grad(i)
+    each(NZ, spread)
+
+    def tail(i):
+        take_input_grad(i)
         send_a(1, i)
 
         @pl.when(i > 0)
         def _():
             send_z(1, i - 1)
 
-    each(NZ, spread)
-    each(NZ, take_input_grad)
+    each(NZ, tail)
     finish(0)
     finish(1)
 
@@ -621,7 +614,7 @@
             pltpu.VMEM((NZ, tok, 4 * rows), BF),
             pltpu.VMEM((1, tok), jnp.int32),
             pltpu.VMEM((2, tok, tok), F32),
-            pltpu.VMEM((2, NZ, 2, 2, rows, half), BF),
+            pltpu.VMEM((NZ, 2, 2, rows, cols), BF),
             pltpu.VMEM((2, 2 * tok, half), F32),
             pltpu.VMEM((2, tok, half), F32),
             pltpu.VMEM((2 * tok, hd), BF),
@@ -645,8 +638,8 @@
             pltpu.VMEM((2, NZ) + block, BF),
             dma((5,)),
             dma((32,)),
-            dma((2, 20)),
-            dma((2, 16)),
+            dma((20,)),
+            dma((16,)),
             dma((2,)),
             dma((2,)),
             dma((12,)),

time: 76.1 us -> 71.1 us (0.934)
  Pallas kernels: 71.4 us -> 66.3 us
    pallas_call x1, Pallas kernels: 71.4 us -> 66.3 us  [kernel_body(): pl.pallas_call(fused, out_shape=(jax.ShapeDtypeStruct(layer_inputs.shape,...]
where the time goes in v9:
time: 71.1 us; the launch traced here: 70.9 us
  Pallas kernels  66.3 us (93%)
  local copies, waits for them, and re-layouts  3.88 us (5%)
    pallas_call x1, Pallas kernels, kernel_body(): pl.pallas_call(fused, out_shape=(jax.ShapeDtypeStruct(layer_inputs.shape,...  66.3 us
    unnamed x4, local copies, waits for them, and re-layouts  3.88 us

profile of v9, /device:TPU:0, one launch (start us, length us, event | category | flops | bytes accessed | tf_op | source)
XLA Modules:
  0.0 70.9 jit_solution(5436688414825372097)
XLA Ops:
  0.6 66.3 %shard_map.59 = (bf16[1,256,4096]{2,1,0:T(8,128)(2,1)}, f32[128,512]{1,0:T(8,128)}) custom-call(bf16[1,256,4096]{2,1,0:T(8,128)(2,1)} %x_hbm.1, s32[1,256]{1,0:T(1,128)} %doc_hbm.1, bf16[128,512]{1,0:T(8,128)(2,1)} %w_hbm.1, bf16[1,256,256]{2,1,0:T(8,128)(2,1)} %do_hbm.1), custom_call_target="tpu_custom_call" | custom-call | tf_op jit(solution)/shard_map/pallas_call | solution.py:601
  67.0 0.0 copy-start
  67.0 3.2 %copy.8 = bf16[1,256,4096]{2,1,0:T(8,128)(2,1)} copy(bf16[1,256,4096]{2,1,0:T(8,128)(2,1)} %get-tuple-element.4) | data formatting | bytes 4194304
  70.2 0.0 copy-done
  70.2 0.7 copy.9
Async XLA Ops:
  67.0 3.2 %copy-start = (f32[128,512]{1,0:T(8,128)S(1)}, f32[128,512]{1,0:T(8,128)}, u32[]{:S(2)}) copy-start(f32[128,512]{1,0:T(8,128)} %get-tuple-element.5) | copy-start | bytes 786436
